TPU v7x, 512 devices: a whole 4x4x16 slice. The times are simulated.
512 devices in a mesh: hi: 16 (over z_lo, core), lo: 32 (over x, y, z_hi).
Axes of the slice: x: 4, y: 4, z: 16 (z_hi: 2, z_lo: 8; z = z_hi * 8 + z_lo), core: 2. Of those that a mesh axis runs over, the one named last changes fastest.
Arguments:
- fields: bfloat16 [2048, 2, 32, 128], P(('hi', 'lo')), may hold values from -6 to 6
- adjoint_in: bfloat16 [2048, 2, 32, 128], P(('hi', 'lo')), may hold values from -6 to 6
- contrast: float32 [2048, 128], P(('hi', 'lo')), may hold values from 0.3 to 3
- coords: bfloat16 [2048, 3, 128], P(('hi', 'lo')), as said below
- neighbours: int32 [2048, 27], P(('hi', 'lo')), may hold values from 0 to 2047, as said below
- partner_perm: int32 [8, 512, 4], P(None, ('hi', 'lo')), may hold values from 0 to 3, each once within a row
- leaf_in: bfloat16 [2048, 64, 128], P(('hi', 'lo')), may hold values from -0.5 to 0.5
- leaf_out: bfloat16 [2048, 64, 128], P(('hi', 'lo')), may hold values from -0.75 to 0.75
- mixing: bfloat16 [8, 2048, 2, 64, 64], P(None, ('hi', 'lo')), may hold values from -0.5 to 0.5
Outputs:
- applied: bfloat16 [2048, 2, 32, 128], P(('hi', 'lo'))
- adjoint_out: bfloat16 [2048, 2, 32, 128], P(('hi', 'lo'))
Inputs may be any that keep to these rules, and one draw needn't show every extreme that they name: `neighbours`: the leaf boxes fill a grid of cells whose Morton codes are 0 to 2048 - 1 (bit t of a code is bit t // 3 of the cell's coordinate along component t % 3). Box g owns one cell c(g), and the 4 boxes of device e own the cells with codes e * 4 to e * 4 + 3, in some order. Row g lists, in some order, the boxes of the 27 cells c(g) + o for o in the finite set (-1, 0, 1)^3, each coordinate clamped to the grid. `coords`: the points of box g lie in the unit cube [c(g), c(g) + 1) of its cell; every coordinate is a multiple of 1/8.
All inputs are finite; a program needn't handle non-finite values.
Results may differ from a plain program's by a relative error of at most 0.015.
Values may be sent and summed in bfloat16 or wider, within the bound.
A program may use at most 64 MiB of HBM per device.

v0:
```python
import math

import jax
import jax.numpy as jnp
from jax import lax
from jax.sharding import PartitionSpec as P

WAVENUMBER = 9.0
SOFTENING = 0.1


def from_behind(block, axis, distance):
    devices = range(lax.axis_size(axis))
    route = [(i - distance, i) for i in devices if i - distance in devices]
    return lax.ppermute(block, axis, route)


def partner(block, axis, bit):
    count = lax.axis_size(axis)
    route = []
    for low in range(count):
        high = low | 1 << bit
        if high != low and high < count:
            route += [(low, high), (high, low)]
    return lax.ppermute(block, axis, route)


def kernel_block(target, sources):
    spread = target[None, :, :, None].astype(jnp.float32) - sources[:, :, None, :].astype(
        jnp.float32
    )
    distance = jnp.sqrt(jnp.sum(spread * spread, axis=1) + SOFTENING * SOFTENING)
    factor = 1.0 / math.sqrt(sources.shape[0] * target.shape[1])
    cosine = factor * jnp.cos(WAVENUMBER * distance) / distance
    sine_part = factor * jnp.sin(WAVENUMBER * distance) / distance
    return jnp.stack([cosine, sine_part], axis=1).astype(jnp.bfloat16)


def near_apply(kernels, sources):
    products = jnp.einsum("kgab,kprb->gpra", kernels, sources, preferred_element_type=jnp.float32)
    return jnp.stack([products[0, 0] - products[1, 1], products[0, 1] + products[1, 0]])


def near_adjoint(kernels, adjoint_box):
    products = jnp.einsum(
        "kgab,pra->kgprb", kernels, adjoint_box, preferred_element_type=jnp.float32
    )
    return jnp.stack(
        [products[:, 0, 0] + products[:, 1, 1], products[:, 0, 1] - products[:, 1, 0]], axis=1
    )


def mix_forward(coefficient, weight):
    return jnp.einsum("brpk,bmk->brpm", coefficient, weight, preferred_element_type=jnp.float32)


def mix_backward(coefficient, weight):
    return jnp.einsum("brpm,bmk->brpk", coefficient, weight, preferred_element_type=jnp.float32)


def grid_extend(grid, layout, mover):
    for dimension in (0, 1, 2):
        axis_pos = 2 - dimension
        amounts, trailing_ones, trailing_zeros = layout[dimension]
        extent = grid.shape[axis_pos]
        bottom = lax.slice_in_dim(grid, 0, 1, axis=axis_pos)
        top = lax.slice_in_dim(grid, extent - 1, extent, axis=axis_pos)
        from_upper = jnp.zeros_like(bottom)
        from_lower = jnp.zeros_like(top)
        for position, amount in enumerate(amounts):
            from_upper = jnp.where(trailing_ones == position, mover(bottom, -amount), from_upper)
            from_lower = jnp.where(trailing_zeros == position, mover(top, amount), from_lower)
        grid = jnp.concatenate([from_lower, grid, from_upper], axis=axis_pos)
    return grid


def grid_fold(grid, layout, mover):
    for dimension in (2, 1, 0):
        axis_pos = 2 - dimension
        amounts, trailing_ones, trailing_zeros = layout[dimension]
        extent = grid.shape[axis_pos]
        bottom = lax.slice_in_dim(grid, 0, 1, axis=axis_pos)
        top = lax.slice_in_dim(grid, extent - 1, extent, axis=axis_pos)
        inner = lax.slice_in_dim(grid, 1, extent - 1, axis=axis_pos)
        onto_top = jnp.zeros_like(bottom)
        onto_bottom = jnp.zeros_like(top)
        for position, amount in enumerate(amounts):
            onto_top = jnp.where(trailing_ones == position, mover(bottom, -amount), onto_top)
            onto_bottom = jnp.where(trailing_zeros == position, mover(top, amount), onto_bottom)
        widths_top = [(0, 0)] * grid.ndim
        widths_top[axis_pos] = (extent - 3, 0)
        widths_bottom = [(0, 0)] * grid.ndim
        widths_bottom[axis_pos] = (0, extent - 3)
        grid = inner + jnp.pad(onto_top, widths_top) + jnp.pad(onto_bottom, widths_bottom)
    return grid


def body(fields, adjoint_in, contrast, coords, neighbours, partner_perm, leaf_in, leaf_out, mixing):
    box_count = fields.shape[0]
    points = fields.shape[3]
    lo_total = lax.axis_size("lo")
    device_total = lax.axis_size("hi") * lo_total
    device = lax.axis_index("hi") * lo_total + lax.axis_index("lo")
    box_bits = box_count.bit_length() - 1
    all_bits = box_bits + device_total.bit_length() - 1
    sizes = []
    extents = []
    anchors = []
    layout = []
    bit_lists = []
    for dimension in range(3):
        local_count = len([t for t in range(box_bits) if t % 3 == dimension])
        global_count = len([t for t in range(all_bits) if t % 3 == dimension])
        device_bits = [t - box_bits for t in range(box_bits, all_bits) if t % 3 == dimension]
        anchor = jnp.zeros((), jnp.int32)
        ones_run = jnp.ones((), jnp.int32)
        zeros_run = jnp.ones((), jnp.int32)
        trailing_ones = jnp.zeros((), jnp.int32)
        trailing_zeros = jnp.zeros((), jnp.int32)
        for bit_place in device_bits:
            value = device >> bit_place & 1
            anchor = anchor + value * (1 << (bit_place + box_bits) // 3)
            ones_run = ones_run * value
            zeros_run = zeros_run * (1 - value)
            trailing_ones = trailing_ones + ones_run
            trailing_zeros = trailing_zeros + zeros_run
        amounts = [
            (1 << device_bits[j]) - sum([1 << device_bits[i] for i in range(j)])
            for j in range(len(device_bits))
        ]
        sizes.append(1 << local_count)
        extents.append(1 << global_count)
        anchors.append(anchor)
        layout.append((amounts, trailing_ones, trailing_zeros))
        bit_lists.append(device_bits)
    wide_x = sizes[0] + 2
    wide_y = sizes[1] + 2
    wide_z = sizes[2] + 2
    wide_count = wide_x * wide_y * wide_z
    cells = jnp.floor(coords[:, :, 0].astype(jnp.float32)).astype(jnp.int32)
    raster_of_box = (
        ((cells[:, 2] - anchors[2]) * sizes[1] + cells[:, 1] - anchors[1]) * sizes[0]
        + cells[:, 0]
        - anchors[0]
    )
    local_slots = jnp.arange(box_count, dtype=jnp.int32)
    placing = raster_of_box[None, :] == local_slots[:, None]
    place_half = placing.astype(jnp.bfloat16)
    place_full = placing.astype(jnp.float32)
    weighted = (contrast[:, None, None, :] * fields.astype(jnp.float32)).astype(jnp.bfloat16)
    slot_rows = jnp.broadcast_to(
        local_slots.astype(jnp.float32)[:, None, None], (box_count, 1, points)
    ).astype(jnp.bfloat16)
    payload = jnp.concatenate([weighted.reshape(box_count, -1, points), coords, slot_rows], axis=1)
    ordered = jnp.einsum(
        "rj,jcx->rcx", place_half, payload, preferred_element_type=jnp.float32
    ).astype(jnp.bfloat16)

    def field_move(layer, amount):
        return from_behind(layer, ("hi", "lo"), amount)

    wide = grid_extend(
        ordered.reshape(sizes[2], sizes[1], sizes[0], -1, points), layout, field_move
    )
    wide_flat = wide.reshape(wide_count, -1, points)
    field_rows = fields.shape[1] * fields.shape[2]
    wide_fields = wide_flat[:, :field_rows].reshape((wide_count,) + fields.shape[1:])
    wide_coords = wide_flat[:, field_rows : field_rows + 3]
    wide_slots = wide_flat[:, field_rows + 3, 0].astype(jnp.float32).astype(jnp.int32)
    wide_index = jnp.arange(wide_count, dtype=jnp.int32)
    wide_local = [
        wide_index % wide_x - 1,
        wide_index // wide_x % wide_y - 1,
        wide_index // (wide_x * wide_y) - 1,
    ]
    inside_all = jnp.ones((wide_count,), jnp.bool_)
    owner = jnp.zeros((wide_count,), jnp.int32)
    for dimension in range(3):
        global_pos = anchors[dimension] + wide_local[dimension]
        inside_all = inside_all & (global_pos >= 0) & (global_pos < extents[dimension])
        clipped_pos = jnp.maximum(global_pos, 0)
        for bit_place in bit_lists[dimension]:
            owner = owner + (clipped_pos >> (bit_place + box_bits) // 3 & 1) * (1 << bit_place)
    wide_id = jnp.where(inside_all, owner * box_count + wide_slots, -1)
    matches = (neighbours[:, :, None] == wide_id[None, None, :]).astype(jnp.int32)
    wide_rows = jnp.sum(matches * wide_index[None, None, :], axis=2)
    zero_wide = jnp.zeros((wide_count,) + fields.shape[1:], jnp.float32)

    def near_only(carry_value, inputs):
        target, rows_here = inputs
        kernels = kernel_block(target, wide_coords[rows_here])
        return (carry_value, near_apply(kernels, wide_fields[rows_here]))

    def back_only(accumulated, inputs):
        target, rows_here, adjoint_box = inputs
        kernels = kernel_block(target, wide_coords[rows_here])
        selector = (rows_here[:, None] == wide_index[None, :]).astype(jnp.float32)
        accumulated = accumulated + jnp.einsum(
            "kt,kprb->tprb",
            selector,
            near_adjoint(kernels, adjoint_box),
            precision=lax.Precision.HIGHEST,
        )
        return (accumulated, None)

    ignored, near_field = lax.scan(near_only, jnp.zeros((), jnp.float32), (coords, wide_rows))
    accumulated, ignored = lax.scan(back_only, zero_wide, (coords, wide_rows, adjoint_in))

    def sums_move(layer, amount):
        return from_behind(layer.astype(jnp.bfloat16), ("hi", "lo"), amount).astype(layer.dtype)

    folded = grid_fold(
        accumulated.reshape((wide_z, wide_y, wide_x) + fields.shape[1:]), layout, sums_move
    )
    near_back = jnp.einsum(
        "rj,rcqx->jcqx", place_full, folded.reshape(fields.shape), precision=lax.Precision.HIGHEST
    )
    lo_count = lax.axis_size("lo").bit_length() - 1
    hi_count = lax.axis_size("hi").bit_length() - 1
    level_total = lo_count - 1 + hi_count
    coefficient = jnp.einsum(
        "bprx,bkx->brpk", weighted, leaf_in, preferred_element_type=jnp.float32
    ).astype(jnp.bfloat16)
    coef_shape = coefficient.shape
    for level_index in range(level_total):
        picker = (partner_perm[level_index, 0][:, None] == local_slots[None, :]).astype(
            jnp.bfloat16
        )
        flattened = coefficient.reshape(box_count, -1)
        if level_index < lo_count - 1:
            partner_block = partner(flattened, "lo", level_index)
        else:
            partner_block = partner(flattened, "hi", level_index - lo_count + 1)
        arrived = (
            jnp.dot(picker, partner_block, preferred_element_type=jnp.float32)
            .astype(jnp.bfloat16)
            .reshape(coef_shape)
        )
        coefficient = (
            mix_forward(coefficient, mixing[level_index, :, 0])
            + mix_forward(arrived, mixing[level_index, :, 1])
        ).astype(jnp.bfloat16)
    far_field = jnp.einsum(
        "brpk,bkx->bprx", coefficient, leaf_out, preferred_element_type=jnp.float32
    )
    applied = (fields.astype(jnp.float32) - (near_field + far_field)).astype(jnp.bfloat16)
    carried_back = jnp.einsum(
        "bprx,bkx->brpk", adjoint_in, leaf_out, preferred_element_type=jnp.float32
    ).astype(jnp.bfloat16)
    for level_index in reversed(range(level_total)):
        picker = (partner_perm[level_index, 0][:, None] == local_slots[None, :]).astype(
            jnp.bfloat16
        )
        partner_term = mix_backward(carried_back, mixing[level_index, :, 1]).astype(jnp.bfloat16)
        placed = jnp.dot(
            picker.T, partner_term.reshape(box_count, -1), preferred_element_type=jnp.float32
        ).astype(jnp.bfloat16)
        if level_index < lo_count - 1:
            returned = partner(placed, "lo", level_index)
        else:
            returned = partner(placed, "hi", level_index - lo_count + 1)
        carried_back = (
            mix_backward(carried_back, mixing[level_index, :, 0])
            + returned.reshape(coef_shape).astype(jnp.float32)
        ).astype(jnp.bfloat16)
    far_back = jnp.einsum(
        "brpk,bkx->bprx", carried_back, leaf_in, preferred_element_type=jnp.float32
    )
    adjoint_out = (
        adjoint_in.astype(jnp.float32) - contrast[:, None, None, :] * (near_back + far_back)
    ).astype(jnp.bfloat16)
    return (applied, adjoint_out)


def solution(mesh):
    in_specs = (
        P(("hi", "lo"), None, None, None),
        P(("hi", "lo"), None, None, None),
        P(("hi", "lo"), None),
        P(("hi", "lo"), None, None),
        P(("hi", "lo"), None),
        P(None, ("hi", "lo"), None),
        P(("hi", "lo"), None, None),
        P(("hi", "lo"), None, None),
        P(None, ("hi", "lo"), None, None, None),
    )
    out_specs = (P(("hi", "lo"), None, None, None), P(("hi", "lo"), None, None, None))
    return jax.shard_map(body, mesh=mesh, in_specs=in_specs, out_specs=out_specs, check_vma=False)
```

profile of v0, /device:TPU:25, one launch (start us, length us, event | category | flops | bytes accessed | tf_op | source)
XLA Modules:
  0.0 674.2 jit_solution(13761022729729755419)
XLA Ops:
  14.1 9.0 %collective-permute-start = (bf16[1,2,1,68,128]{4,2,1,3,0:T(2,128)(2,1)S(1)}, bf16[1,2,1,68,128]{4,2,1,3,0:T(2,128)(2,1)S(1)}, u32[]{:S(2)}, u32[]{:S(2)}) collective-permute-start(bf16[1,2,1,68,128]{4,2,1,3,0:T(2,128)(2,1)S(1)} %get-tuple-element.192), channel_id=1, source_target_pairs={{0,110},{1,111},{2,112},{3,113},{4,114},{5,115},{6,116},{7,117},{8... | collective-permute-start | bytes 104456 | tf_op jit(solution)/shard_map/ppermute | solution.py:15
  24.4 15.4 %collective-permute-start.18 = (bf16[4,4096]{1,0:T(4,128)(2,1)S(1)}, bf16[4,4096]{1,0:T(4,128)(2,1)S(1)}, u32[]{:S(2)}, u32[]{:S(2)}) collective-permute-start(bf16[4,4096]{1,0:T(4,128)(2,1)S(1)} %reshape.539), channel_id=1, source_target_pairs={{0,1},{1,0},{2,3},{3,2},{4,5},{5,4},{6,7},{7,6},{8,9},{9,8},{10,11... | collective-permute-start | bytes 98312 | tf_op jit(solution)/shard_map/ppermute | solution.py:25
  80.9 13.3 %collective-permute-start.6 = (bf16[1,1,4,68,128]{4,2,1,3,0:T(4,128)(2,1)}, bf16[1,1,4,68,128]{4,2,1,3,0:T(4,128)(2,1)}, u32[]{:S(2)}, u32[]{:S(2)}) collective-permute-start(bf16[1,1,4,68,128]{4,2,1,3,0:T(4,128)(2,1)} %get-tuple-element.188), channel_id=1, source_target_pairs={{0,220},{1,221},{2,222},{3,223},{4,224},{5,225},{6,226},{7,227},{8... | collective-permute-start | bytes 208904 | tf_op jit(solution)/shard_map/ppermute | solution.py:15
  124.9 11.5 %collective-permute-start.16 = (bf16[1,4,4,68,128]{4,2,1,3,0:T(4,128)(2,1)}, bf16[1,4,4,68,128]{4,2,1,3,0:T(4,128)(2,1)}, u32[]{:S(2)}, u32[]{:S(2)}) collective-permute-start(bf16[1,4,4,68,128]{4,2,1,3,0:T(4,128)(2,1)} %pad_maximum_fusion.2), channel_id=1, source_target_pairs={{7,0},{8,1},{9,2},{10,3},{11,4},{12,5},{13,6},{14,7},{15,8},{16,9}... | collective-permute-start | bytes 835592 | tf_op jit(solution)/shard_map/ppermute | solution.py:15
  140.9 15.3 %collective-permute-start.12 = (bf16[1,4,4,68,128]{4,2,1,3,0:T(4,128)(2,1)}, bf16[1,4,4,68,128]{4,2,1,3,0:T(4,128)(2,1)}, u32[]{:S(2)}, u32[]{:S(2)}) collective-permute-start(bf16[1,4,4,68,128]{4,2,1,3,0:T(4,128)(2,1)} %pad_maximum_fusion.2), channel_id=1, source_target_pairs={{0,55},{1,56},{2,57},{3,58},{4,59},{5,60},{6,61},{7,62},{8,63},{9,... | collective-permute-start | bytes 835592 | tf_op jit(solution)/shard_map/ppermute | solution.py:15
  171.3 39.2 %collective-permute-done.23 = bf16[4,4096]{1,0:T(4,128)(2,1)} collective-permute-done((bf16[4,4096]{1,0:T(4,128)(2,1)S(1)}, bf16[4,4096]{1,0:T(4,128)(2,1)}, u32[]{:S(2)}, u32[]{:S(2)}) %collective-permute-start.23) | collective-permute-done | bytes 32800 | tf_op jit(solution)/shard_map/ppermute | solution.py:25
  218.2 30.2 %collective-permute-start.50 = (bf16[4,4096]{1,0:T(4,128)(2,1)}, bf16[4,4096]{1,0:T(4,128)(2,1)}, u32[]{:S(2)}, u32[]{:S(2)}) collective-permute-start(bf16[4,4096]{1,0:T(4,128)(2,1)} %convolution_convert_fusion.1), channel_id=1, source_target_pairs={{0,2},{2,0},{1,3},{3,1},{4,6},{6,4},{5,7},{7,5},{8,10},{10,8},{9,1... | collective-permute-start | bytes 98312 | tf_op jit(solution)/shard_map/ppermute | solution.py:25
  257.8 19.7 %collective-permute-start.14 = (bf16[1,4,4,68,128]{4,2,1,3,0:T(4,128)(2,1)}, bf16[1,4,4,68,128]{4,2,1,3,0:T(4,128)(2,1)}, u32[]{:S(2)}, u32[]{:S(2)}) collective-permute-start(bf16[1,4,4,68,128]{4,2,1,3,0:T(4,128)(2,1)} %pad_maximum_fusion.2), channel_id=1, source_target_pairs={{0,1},{1,2},{2,3},{3,4},{4,5},{5,6},{6,7},{7,8},{8,9},{9,10},{10,1... | collective-permute-start | bytes 835592 | tf_op jit(solution)/shard_map/ppermute | solution.py:15
  281.9 22.2 %collective-permute-done.14 = bf16[1,4,4,68,128]{4,2,1,3,0:T(4,128)(2,1)} collective-permute-done((bf16[1,4,4,68,128]{4,2,1,3,0:T(4,128)(2,1)}, bf16[1,4,4,68,128]{4,2,1,3,0:T(4,128)(2,1)}, u32[]{:S(2)}, u32[]{:S(2)}) %collective-permute-start.14) | collective-permute-done | bytes 278560 | tf_op jit(solution)/shard_map/ppermute | solution.py:15
  306.9 45.1 %while.22 = (s32[]{:T(128)}, f32[48,2,32,128]{3,0,2,1:T(8,128)S(1)}, s32[4,27]{1,0:T(4,128)S(1)}, bf16[4,2,32,128]{3,2,1,0:T(8,128)(2,1)S(1)}, bf16[4,3,128]{2,1...) while((s32[]{:T(128)}, f32[48,2,32,128]{3,0,2,1:T(8,128)S(1)}, ...), condition=%wide.region_6.7_spmd.clone, body=%wide.region_4.6_spmd.clone.sunk | while | flops 252506976 | bytes 17471852 | solution.py:207
  352.9 9.7 %collective-permute-start.31 = (bf16[1,4,4,2,32,128]{5,2,1,4,3,0:T(4,128)(2,1)}, bf16[1,4,4,2,32,128]{5,2,1,4,3,0:T(4,128)(2,1)S(1)}, u32[]{:S(2)}, u32[]{:S(2)}) collective-permute-start(bf16[1,4,4,2,32,128]{5,2,1,4,3,0:T(4,128)(2,1)} %bitcast.77), channel_id=1, source_target_pairs={{0,1},{1,2},{2,3},{3,4},{4,5},{5,6},{6,7},{7,8},{8,9},{9,10},{10,1... | collective-permute-start | bytes 786440 | tf_op jit(solution)/shard_map/ppermute | solution.py:15
  364.1 15.6 %collective-permute-start.51 = (bf16[4,4096]{1,0:T(4,128)(2,1)S(1)}, bf16[4,4096]{1,0:T(4,128)(2,1)S(1)}, u32[]{:S(2)}, u32[]{:S(2)}) collective-permute-start(bf16[4,4096]{1,0:T(4,128)(2,1)S(1)} %convolution_convert_fusion), channel_id=1, source_target_pairs={{0,1},{1,0},{2,3},{3,2},{4,5},{5,4},{6,7},{7,6},{8,9},{9,8},{10,11... | collective-permute-start | bytes 98312 | tf_op jit(solution)/shard_map/ppermute | solution.py:25
  379.7 8.9 %collective-permute-start.30 = (bf16[1,4,4,2,32,128]{5,2,1,4,3,0:T(4,128)(2,1)}, bf16[1,4,4,2,32,128]{5,2,1,4,3,0:T(4,128)(2,1)}, u32[]{:S(2)}, u32[]{:S(2)}) collective-permute-start(bf16[1,4,4,2,32,128]{5,2,1,4,3,0:T(4,128)(2,1)} %bitcast.77), channel_id=1, source_target_pairs={{0,7},{1,8},{2,9},{3,10},{4,11},{5,12},{6,13},{7,14},{8,15},{9,16}... | collective-permute-start | bytes 786440 | tf_op jit(solution)/shard_map/ppermute | solution.py:15
  388.6 33.0 %collective-permute-start.29 = (bf16[1,4,4,2,32,128]{5,2,1,4,3,0:T(4,128)(2,1)}, bf16[1,4,4,2,32,128]{5,2,1,4,3,0:T(4,128)(2,1)}, u32[]{:S(2)}, u32[]{:S(2)}) collective-permute-start(bf16[1,4,4,2,32,128]{5,2,1,4,3,0:T(4,128)(2,1)} %bitcast.77), channel_id=1, source_target_pairs={{0,55},{1,56},{2,57},{3,58},{4,59},{5,60},{6,61},{7,62},{8,63},{9,... | collective-permute-start | bytes 786440 | tf_op jit(solution)/shard_map/ppermute | solution.py:15
  425.8 11.3 %collective-permute-start.27 = (bf16[1,4,4,2,32,128]{5,2,1,4,3,0:T(4,128)(2,1)}, bf16[1,4,4,2,32,128]{5,2,1,4,3,0:T(4,128)(2,1)}, u32[]{:S(2)}, u32[]{:S(2)}) collective-permute-start(bf16[1,4,4,2,32,128]{5,2,1,4,3,0:T(4,128)(2,1)} %bitcast.460), channel_id=1, source_target_pairs={{7,0},{8,1},{9,2},{10,3},{11,4},{12,5},{13,6},{14,7},{15,8},{16,9}... | collective-permute-start | bytes 786440 | tf_op jit(solution)/shard_map/ppermute | solution.py:15
  442.7 24.0 %collective-permute-done.29 = bf16[1,4,4,2,32,128]{5,2,1,4,3,0:T(4,128)(2,1)} collective-permute-done((bf16[1,4,4,2,32,128]{5,2,1,4,3,0:T(4,128)(2,1)}, bf16[1,4,4,2,32,128]{5,2,1,4,3,0:T(4,128)(2,1)}, u32[]{:S(2)}, u32[]{:S(2)}) %collective-permute-start.29) | collective-permute-done | bytes 262176 | tf_op jit(solution)/shard_map/ppermute | solution.py:15
  466.7 14.5 %collective-permute-done.28 = bf16[1,4,4,2,32,128]{5,2,1,4,3,0:T(4,128)(2,1)} collective-permute-done((bf16[1,4,4,2,32,128]{5,2,1,4,3,0:T(4,128)(2,1)}, bf16[1,4,4,2,32,128]{5,2,1,4,3,0:T(4,128)(2,1)}, u32[]{:S(2)}, u32[]{:S(2)}) %collective-permute-start.28) | collective-permute-done | bytes 262176 | tf_op jit(solution)/shard_map/ppermute | solution.py:15
  481.3 19.4 %collective-permute-done.26 = bf16[1,4,4,2,32,128]{5,2,1,4,3,0:T(4,128)(2,1)} collective-permute-done((bf16[1,4,4,2,32,128]{5,2,1,4,3,0:T(4,128)(2,1)}, bf16[1,4,4,2,32,128]{5,2,1,4,3,0:T(4,128)(2,1)}, u32[]{:S(2)}, u32[]{:S(2)}) %collective-permute-start.26) | collective-permute-done | bytes 262176 | tf_op jit(solution)/shard_map/ppermute | solution.py:15
  505.9 32.6 %collective-permute-start.36 = (bf16[1,1,4,2,32,128]{5,2,1,4,3,0:T(4,128)(2,1)}, bf16[1,1,4,2,32,128]{5,2,1,4,3,0:T(4,128)(2,1)}, u32[]{:S(2)}, u32[]{:S(2)}) collective-permute-start(bf16[1,1,4,2,32,128]{5,2,1,4,3,0:T(4,128)(2,1)} %get-tuple-element.187), channel_id=1, source_target_pairs={{0,28},{1,29},{2,30},{3,31},{4,32},{5,33},{6,34},{7,35},{8,36},{9,... | collective-permute-start | bytes 196616 | tf_op jit(solution)/shard_map/ppermute | solution.py:15
  540.4 39.7 %while.21 = (s32[]{:T(128)}, f32[4,2,32,128]{3,2,1,0:T(8,128)S(1)}, s32[4,27]{1,0:T(4,128)S(1)}, bf16[48,2,32,128]{3,2,1,0:T(8,128)(2,1)S(1)}, bf16[4,3,128]{2,1...) while((s32[]{:T(128)}, f32[4,2,32,128]{3,2,1,0:T(8,128)S(1)}, s32[4,27]{1,0:T(4,128)S(1)}, ...), condition=%wide.region_3.4_spmd, body=%wide.region_1.3_spmd.sunk | while | flops 123891280 | bytes 8788093 | solution.py:206
  580.1 11.0 %collective-permute-start.34 = (bf16[1,1,4,2,32,128]{5,2,1,4,3,0:T(4,128)(2,1)}, bf16[1,1,4,2,32,128]{5,2,1,4,3,0:T(4,128)(2,1)S(1)}, u32[]{:S(2)}, u32[]{:S(2)}) collective-permute-start(bf16[1,1,4,2,32,128]{5,2,1,4,3,0:T(4,128)(2,1)} %get-tuple-element.186), channel_id=1, source_target_pairs={{4,0},{5,1},{6,2},{7,3},{8,4},{9,5},{10,6},{11,7},{12,8},{13,9},{1... | collective-permute-start | bytes 196616 | tf_op jit(solution)/shard_map/ppermute | solution.py:15
  599.7 9.9 %collective-permute-done.32 = bf16[1,1,4,2,32,128]{5,2,1,4,3,0:T(4,128)(2,1)S(1)} collective-permute-done((bf16[1,1,4,2,32,128]{5,2,1,4,3,0:T(4,128)(2,1)}, bf16[1,1,4,2,32,128]{5,2,1,4,3,0:T(4,128)(2,1)S(1)}, u32[]{:S(2)}, u32[]{:S(2)}) %collective-permute-start.32) | collective-permute-done | bytes 65568 | tf_op jit(solution)/shard_map/ppermute | solution.py:15
  612.7 24.1 %collective-permute-start.42 = (bf16[1,2,1,2,32,128]{5,2,1,4,3,0:T(2,128)(2,1)S(1)}, bf16[1,2,1,2,32,128]{5,2,1,4,3,0:T(2,128)(2,1)S(1)}, u32[]{:S(2)}, u32[]{:S(2)}) collective-permute-start(bf16[1,2,1,2,32,128]{5,2,1,4,3,0:T(2,128)(2,1)S(1)} %get-tuple-element.191), channel_id=1, source_target_pairs={{0,14},{1,15},{2,16},{3,17},{4,18},{5,19},{6,20},{7,21},{8,22},{9,... | collective-permute-start | bytes 98312 | tf_op jit(solution)/shard_map/ppermute | solution.py:15
  636.9 18.7 %collective-permute-start.41 = (bf16[1,2,1,2,32,128]{5,2,1,4,3,0:T(2,128)(2,1)S(1)}, bf16[1,2,1,2,32,128]{5,2,1,4,3,0:T(2,128)(2,1)S(1)}, u32[]{:S(2)}, u32[]{:S(2)}) collective-permute-start(bf16[1,2,1,2,32,128]{5,2,1,4,3,0:T(2,128)(2,1)S(1)} %get-tuple-element.191), channel_id=1, source_target_pairs={{0,110},{1,111},{2,112},{3,113},{4,114},{5,115},{6,116},{7,117},{8... | collective-permute-start | bytes 98312 | tf_op jit(solution)/shard_map/ppermute | solution.py:15
  (368 shorter events, 262.7 us)
Async XLA Ops:
  4.5 54.3 %collective-permute-start.3 = (bf16[1,2,1,68,128]{4,2,1,3,0:T(2,128)(2,1)}, bf16[1,2,1,68,128]{4,2,1,3,0:T(2,128)(2,1)S(1)}, u32[]{:S(2)}, u32[]{:S(2)}) collective-permute-start(bf16[1,2,1,68,128]{4,2,1,3,0:T(2,128)(2,1)} %get-tuple-element.193), channel_id=1, source_target_pairs={{110,0},{111,1},{112,2},{113,3},{114,4},{115,5},{116,6},{117,7},{1... | collective-permute-start | bytes 104456 | tf_op jit(solution)/shard_map/ppermute | solution.py:15
  5.8 55.2 %collective-permute-start.4 = (bf16[1,2,1,68,128]{4,2,1,3,0:T(2,128)(2,1)}, bf16[1,2,1,68,128]{4,2,1,3,0:T(2,128)(2,1)}, u32[]{:S(2)}, u32[]{:S(2)}) collective-permute-start(bf16[1,2,1,68,128]{4,2,1,3,0:T(2,128)(2,1)} %get-tuple-element.193), channel_id=1, source_target_pairs={{14,0},{15,1},{16,2},{17,3},{18,4},{19,5},{20,6},{21,7},{22,8},{23... | collective-permute-start | bytes 104456 | tf_op jit(solution)/shard_map/ppermute | solution.py:15
  10.4 53.7 %collective-permute-start.5 = (bf16[1,2,1,68,128]{4,2,1,3,0:T(2,128)(2,1)}, bf16[1,2,1,68,128]{4,2,1,3,0:T(2,128)(2,1)}, u32[]{:S(2)}, u32[]{:S(2)}) collective-permute-start(bf16[1,2,1,68,128]{4,2,1,3,0:T(2,128)(2,1)} %get-tuple-element.193), channel_id=1, source_target_pairs={{2,0},{3,1},{4,2},{5,3},{6,4},{7,5},{8,6},{9,7},{10,8},{11,9},{12,... | collective-permute-start | bytes 104456 | tf_op jit(solution)/shard_map/ppermute | solution.py:15
  14.1 54.7 %collective-permute-start = (bf16[1,2,1,68,128]{4,2,1,3,0:T(2,128)(2,1)S(1)}, bf16[1,2,1,68,128]{4,2,1,3,0:T(2,128)(2,1)S(1)}, u32[]{:S(2)}, u32[]{:S(2)}) collective-permute-start(bf16[1,2,1,68,128]{4,2,1,3,0:T(2,128)(2,1)S(1)} %get-tuple-element.192), channel_id=1, source_target_pairs={{0,110},{1,111},{2,112},{3,113},{4,114},{5,115},{6,116},{7,117},{8... | collective-permute-start | bytes 104456 | tf_op jit(solution)/shard_map/ppermute | solution.py:15
  71.3 44.4 %collective-permute-start.10 = (bf16[1,1,4,68,128]{4,2,1,3,0:T(4,128)(2,1)}, bf16[1,1,4,68,128]{4,2,1,3,0:T(4,128)(2,1)}, u32[]{:S(2)}, u32[]{:S(2)}) collective-permute-start(bf16[1,1,4,68,128]{4,2,1,3,0:T(4,128)(2,1)} %get-tuple-element.189), channel_id=1, source_target_pairs={{28,0},{29,1},{30,2},{31,3},{32,4},{33,5},{34,6},{35,7},{36,8},{37... | collective-permute-start | bytes 208904 | tf_op jit(solution)/shard_map/ppermute | solution.py:15
  123.6 134.2 %collective-permute-start.15 = (bf16[1,4,4,68,128]{4,2,1,3,0:T(4,128)(2,1)}, bf16[1,4,4,68,128]{4,2,1,3,0:T(4,128)(2,1)}, u32[]{:S(2)}, u32[]{:S(2)}) collective-permute-start(bf16[1,4,4,68,128]{4,2,1,3,0:T(4,128)(2,1)} %pad_maximum_fusion.2), channel_id=1, source_target_pairs={{55,0},{56,1},{57,2},{58,3},{59,4},{60,5},{61,6},{62,7},{63,8},{64... | collective-permute-start | bytes 835592 | tf_op jit(solution)/shard_map/ppermute | solution.py:15
  124.9 153.6 %collective-permute-start.16 = (bf16[1,4,4,68,128]{4,2,1,3,0:T(4,128)(2,1)}, bf16[1,4,4,68,128]{4,2,1,3,0:T(4,128)(2,1)}, u32[]{:S(2)}, u32[]{:S(2)}) collective-permute-start(bf16[1,4,4,68,128]{4,2,1,3,0:T(4,128)(2,1)} %pad_maximum_fusion.2), channel_id=1, source_target_pairs={{7,0},{8,1},{9,2},{10,3},{11,4},{12,5},{13,6},{14,7},{15,8},{16,9}... | collective-permute-start | bytes 835592 | tf_op jit(solution)/shard_map/ppermute | solution.py:15
  136.4 144.2 %collective-permute-start.17 = (bf16[1,4,4,68,128]{4,2,1,3,0:T(4,128)(2,1)}, bf16[1,4,4,68,128]{4,2,1,3,0:T(4,128)(2,1)}, u32[]{:S(2)}, u32[]{:S(2)}) collective-permute-start(bf16[1,4,4,68,128]{4,2,1,3,0:T(4,128)(2,1)} %pad_maximum_fusion.2), channel_id=1, source_target_pairs={{1,0},{2,1},{3,2},{4,3},{5,4},{6,5},{7,6},{8,7},{9,8},{10,9},{11,1... | collective-permute-start | bytes 835592 | tf_op jit(solution)/shard_map/ppermute | solution.py:15
  140.9 141.0 %collective-permute-start.12 = (bf16[1,4,4,68,128]{4,2,1,3,0:T(4,128)(2,1)}, bf16[1,4,4,68,128]{4,2,1,3,0:T(4,128)(2,1)}, u32[]{:S(2)}, u32[]{:S(2)}) collective-permute-start(bf16[1,4,4,68,128]{4,2,1,3,0:T(4,128)(2,1)} %pad_maximum_fusion.2), channel_id=1, source_target_pairs={{0,55},{1,56},{2,57},{3,58},{4,59},{5,60},{6,61},{7,62},{8,63},{9,... | collective-permute-start | bytes 835592 | tf_op jit(solution)/shard_map/ppermute | solution.py:15
  167.7 42.8 %collective-permute-start.23 = (bf16[4,4096]{1,0:T(4,128)(2,1)S(1)}, bf16[4,4096]{1,0:T(4,128)(2,1)}, u32[]{:S(2)}, u32[]{:S(2)}) collective-permute-start(bf16[4,4096]{1,0:T(4,128)(2,1)S(1)} %reshape.549), channel_id=1, source_target_pairs={{0,64},{64,0},{32,96},{96,32},{128,192},{192,128},{160,224},{224,1... | collective-permute-start | bytes 98312 | tf_op jit(solution)/shard_map/ppermute | solution.py:25
  257.8 46.3 %collective-permute-start.14 = (bf16[1,4,4,68,128]{4,2,1,3,0:T(4,128)(2,1)}, bf16[1,4,4,68,128]{4,2,1,3,0:T(4,128)(2,1)}, u32[]{:S(2)}, u32[]{:S(2)}) collective-permute-start(bf16[1,4,4,68,128]{4,2,1,3,0:T(4,128)(2,1)} %pad_maximum_fusion.2), channel_id=1, source_target_pairs={{0,1},{1,2},{2,3},{3,4},{4,5},{5,6},{6,7},{7,8},{8,9},{9,10},{10,1... | collective-permute-start | bytes 835592 | tf_op jit(solution)/shard_map/ppermute | solution.py:15
  278.6 143.0 %collective-permute-start.25 = (bf16[4,4096]{1,0:T(4,128)(2,1)}, bf16[4,4096]{1,0:T(4,128)(2,1)}, u32[]{:S(2)}, u32[]{:S(2)}) collective-permute-start(bf16[4,4096]{1,0:T(4,128)(2,1)} %reshape.553), channel_id=1, source_target_pairs={{0,256},{256,0},{32,288},{288,32},{64,320},{320,64},{96,352},{352,... | collective-permute-start | bytes 98312 | tf_op jit(solution)/shard_map/ppermute | solution.py:25
  352.9 84.1 %collective-permute-start.31 = (bf16[1,4,4,2,32,128]{5,2,1,4,3,0:T(4,128)(2,1)}, bf16[1,4,4,2,32,128]{5,2,1,4,3,0:T(4,128)(2,1)S(1)}, u32[]{:S(2)}, u32[]{:S(2)}) collective-permute-start(bf16[1,4,4,2,32,128]{5,2,1,4,3,0:T(4,128)(2,1)} %bitcast.77), channel_id=1, source_target_pairs={{0,1},{1,2},{2,3},{3,4},{4,5},{5,6},{6,7},{7,8},{8,9},{9,10},{10,1... | collective-permute-start | bytes 786440 | tf_op jit(solution)/shard_map/ppermute | solution.py:15
  364.1 61.6 %collective-permute-start.51 = (bf16[4,4096]{1,0:T(4,128)(2,1)S(1)}, bf16[4,4096]{1,0:T(4,128)(2,1)S(1)}, u32[]{:S(2)}, u32[]{:S(2)}) collective-permute-start(bf16[4,4096]{1,0:T(4,128)(2,1)S(1)} %convolution_convert_fusion), channel_id=1, source_target_pairs={{0,1},{1,0},{2,3},{3,2},{4,5},{5,4},{6,7},{7,6},{8,9},{9,8},{10,11... | collective-permute-start | bytes 98312 | tf_op jit(solution)/shard_map/ppermute | solution.py:25
  379.7 63.0 %collective-permute-start.30 = (bf16[1,4,4,2,32,128]{5,2,1,4,3,0:T(4,128)(2,1)}, bf16[1,4,4,2,32,128]{5,2,1,4,3,0:T(4,128)(2,1)}, u32[]{:S(2)}, u32[]{:S(2)}) collective-permute-start(bf16[1,4,4,2,32,128]{5,2,1,4,3,0:T(4,128)(2,1)} %bitcast.77), channel_id=1, source_target_pairs={{0,7},{1,8},{2,9},{3,10},{4,11},{5,12},{6,13},{7,14},{8,15},{9,16}... | collective-permute-start | bytes 786440 | tf_op jit(solution)/shard_map/ppermute | solution.py:15
  388.6 78.1 %collective-permute-start.29 = (bf16[1,4,4,2,32,128]{5,2,1,4,3,0:T(4,128)(2,1)}, bf16[1,4,4,2,32,128]{5,2,1,4,3,0:T(4,128)(2,1)}, u32[]{:S(2)}, u32[]{:S(2)}) collective-permute-start(bf16[1,4,4,2,32,128]{5,2,1,4,3,0:T(4,128)(2,1)} %bitcast.77), channel_id=1, source_target_pairs={{0,55},{1,56},{2,57},{3,58},{4,59},{5,60},{6,61},{7,62},{8,63},{9,... | collective-permute-start | bytes 786440 | tf_op jit(solution)/shard_map/ppermute | solution.py:15
  421.6 59.7 %collective-permute-start.28 = (bf16[1,4,4,2,32,128]{5,2,1,4,3,0:T(4,128)(2,1)}, bf16[1,4,4,2,32,128]{5,2,1,4,3,0:T(4,128)(2,1)}, u32[]{:S(2)}, u32[]{:S(2)}) collective-permute-start(bf16[1,4,4,2,32,128]{5,2,1,4,3,0:T(4,128)(2,1)} %bitcast.459), channel_id=1, source_target_pairs={{1,0},{2,1},{3,2},{4,3},{5,4},{6,5},{7,6},{8,7},{9,8},{10,9},{11,1... | collective-permute-start | bytes 786440 | tf_op jit(solution)/shard_map/ppermute | solution.py:15
  425.8 55.5 %collective-permute-start.27 = (bf16[1,4,4,2,32,128]{5,2,1,4,3,0:T(4,128)(2,1)}, bf16[1,4,4,2,32,128]{5,2,1,4,3,0:T(4,128)(2,1)}, u32[]{:S(2)}, u32[]{:S(2)}) collective-permute-start(bf16[1,4,4,2,32,128]{5,2,1,4,3,0:T(4,128)(2,1)} %bitcast.460), channel_id=1, source_target_pairs={{7,0},{8,1},{9,2},{10,3},{11,4},{12,5},{13,6},{14,7},{15,8},{16,9}... | collective-permute-start | bytes 786440 | tf_op jit(solution)/shard_map/ppermute | solution.py:15
  437.1 63.6 %collective-permute-start.26 = (bf16[1,4,4,2,32,128]{5,2,1,4,3,0:T(4,128)(2,1)}, bf16[1,4,4,2,32,128]{5,2,1,4,3,0:T(4,128)(2,1)}, u32[]{:S(2)}, u32[]{:S(2)}) collective-permute-start(bf16[1,4,4,2,32,128]{5,2,1,4,3,0:T(4,128)(2,1)} %bitcast.461), channel_id=1, source_target_pairs={{55,0},{56,1},{57,2},{58,3},{59,4},{60,5},{61,6},{62,7},{63,8},{64... | collective-permute-start | bytes 786440 | tf_op jit(solution)/shard_map/ppermute | solution.py:15
  504.0 93.5 %collective-permute-start.37 = (bf16[1,1,4,2,32,128]{5,2,1,4,3,0:T(4,128)(2,1)}, bf16[1,1,4,2,32,128]{5,2,1,4,3,0:T(4,128)(2,1)S(1)}, u32[]{:S(2)}, u32[]{:S(2)}) collective-permute-start(bf16[1,1,4,2,32,128]{5,2,1,4,3,0:T(4,128)(2,1)} %get-tuple-element.187), channel_id=1, source_target_pairs={{0,4},{1,5},{2,6},{3,7},{4,8},{5,9},{6,10},{7,11},{8,12},{9,13},{1... | collective-permute-start | bytes 196616 | tf_op jit(solution)/shard_map/ppermute | solution.py:15
  505.9 92.9 %collective-permute-start.36 = (bf16[1,1,4,2,32,128]{5,2,1,4,3,0:T(4,128)(2,1)}, bf16[1,1,4,2,32,128]{5,2,1,4,3,0:T(4,128)(2,1)}, u32[]{:S(2)}, u32[]{:S(2)}) collective-permute-start(bf16[1,1,4,2,32,128]{5,2,1,4,3,0:T(4,128)(2,1)} %get-tuple-element.187), channel_id=1, source_target_pairs={{0,28},{1,29},{2,30},{3,31},{4,32},{5,33},{6,34},{7,35},{8,36},{9,... | collective-permute-start | bytes 196616 | tf_op jit(solution)/shard_map/ppermute | solution.py:15
  538.5 60.3 %collective-permute-start.35 = (bf16[1,1,4,2,32,128]{5,2,1,4,3,0:T(4,128)(2,1)}, bf16[1,1,4,2,32,128]{5,2,1,4,3,0:T(4,128)(2,1)}, u32[]{:S(2)}, u32[]{:S(2)}) collective-permute-start(bf16[1,1,4,2,32,128]{5,2,1,4,3,0:T(4,128)(2,1)} %get-tuple-element.187), channel_id=1, source_target_pairs={{0,220},{1,221},{2,222},{3,223},{4,224},{5,225},{6,226},{7,227},{8... | collective-permute-start | bytes 196616 | tf_op jit(solution)/shard_map/ppermute | solution.py:15
  610.8 50.4 %collective-permute-start.43 = (bf16[1,2,1,2,32,128]{5,2,1,4,3,0:T(2,128)(2,1)S(1)}, bf16[1,2,1,2,32,128]{5,2,1,4,3,0:T(2,128)(2,1)S(1)}, u32[]{:S(2)}, u32[]{:S(2)}) collective-permute-start(bf16[1,2,1,2,32,128]{5,2,1,4,3,0:T(2,128)(2,1)S(1)} %get-tuple-element.191), channel_id=1, source_target_pairs={{0,2},{1,3},{2,4},{3,5},{4,6},{5,7},{6,8},{7,9},{8,10},{9,11},{10,... | collective-permute-start | bytes 98312 | tf_op jit(solution)/shard_map/ppermute | solution.py:15
  612.7 49.8 %collective-permute-start.42 = (bf16[1,2,1,2,32,128]{5,2,1,4,3,0:T(2,128)(2,1)S(1)}, bf16[1,2,1,2,32,128]{5,2,1,4,3,0:T(2,128)(2,1)S(1)}, u32[]{:S(2)}, u32[]{:S(2)}) collective-permute-start(bf16[1,2,1,2,32,128]{5,2,1,4,3,0:T(2,128)(2,1)S(1)} %get-tuple-element.191), channel_id=1, source_target_pairs={{0,14},{1,15},{2,16},{3,17},{4,18},{5,19},{6,20},{7,21},{8,22},{9,... | collective-permute-start | bytes 98312 | tf_op jit(solution)/shard_map/ppermute | solution.py:15
  (50 other events, 1671.3 us)
where the time goes:
time: 684 us; the launch traced here: 674 us
  starting transfers between devices  377 us (55%)
  waiting for transfers between devices  153 us (22%)
  other arithmetic  77.5 us (11%)
  matrix products  37.7 us (6%)
  local copies, waits for them, and re-layouts  26.3 us (4%)
    ppermute x36, starting transfers between devices, from_behind(): return lax.ppermute(block, axis, route)  282 us
    ppermute x36, waiting for transfers between devices, from_behind(): return lax.ppermute(block, axis, route)  99.1 us
    ppermute x16, starting transfers between devices, partner(): return lax.ppermute(block, axis, route)  94.2 us
    another operation x11, other arithmetic  61.3 us
    ppermute x16, waiting for transfers between devices, partner(): return lax.ppermute(block, axis, route)  54.1 us
  transfers between devices with their start and end apart: 52, of which 16 were waited for; matrix products, arithmetic and copies ran while one was open for 19% of the time, Pallas kernels for 0%

commit v1 on v0

v1 whole, which is shorter than its diff:
```python
import functools
import math

import jax
import jax.numpy as jnp
import numpy as np
from jax import lax
from jax.experimental import pallas as pl
from jax.experimental.pallas import tpu as pltpu
from jax.sharding import PartitionSpec as P

WAVENUMBER = 9.0
SOFTENING = 0.1
MESH = pl.DeviceIdType.MESH
ROWS = 144
MAGIC = 12582912.0
BF = jnp.bfloat16
F32 = jnp.float32
NT = (((1,), (1,)), ((), ()))
TN = (((0,), (0,)), ((), ()))


def fit(function, degree):
    nodes = 0.125 * (1.0 - np.cos(np.pi * (np.arange(400) + 0.5) / 400))
    poly = np.polynomial.chebyshev.Chebyshev.fit(nodes, function(nodes), degree, domain=[0, 0.25])
    return [float(c) for c in poly.convert(kind=np.polynomial.Polynomial).coef]


CYCLES = WAVENUMBER / (2 * math.pi)
COS_POLY = fit(lambda s: np.cos(2 * np.pi * np.sqrt(s)), 4)
SIN_POLY = fit(lambda s: np.sin(2 * np.pi * np.sqrt(s)) / np.sqrt(s), 3)


def horner(coefs, s):
    value = coefs[-1] * s + coefs[-2]
    for c in coefs[-3::-1]:
        value = value * s + c
    return value


def oscillation(squared, scale):
    w = squared * (CYCLES * CYCLES / 64.0) + CYCLES * CYCLES * SOFTENING * SOFTENING
    r = lax.rsqrt(w)
    y = w * r
    f = y - ((y + MAGIC) - MAGIC)
    s = f * f
    amp = scale * CYCLES
    real = horner([amp * c for c in COS_POLY], s) * r
    imag = horner([amp * c for c in SIN_POLY], s) * (f * r)
    return real.astype(BF), imag.astype(BF)


def spread(value, bits):
    total = 0
    for place, bit in enumerate(bits):
        total = total + (value // (1 << place)) % 2 * (1 << bit)
    return total


def dot(a, b, dims=None):
    if dims is None:
        return jnp.dot(a, b, preferred_element_type=F32)
    return lax.dot_general(a, b, dims, preferred_element_type=F32)


def kernel(
    n_hi, n_lo, scale,
    cell_ref, perm_ref, fields_ref, adj_ref, contrast_ref, coords_ref, lin_ref, lout_ref, mix_ref,
    out_ref, adj_out_ref,
    grid, tgt, acc, wbuf, ll_in, ll_out, blocks, fsend, bsend, brecv, carry,
    send_sem, recv_sem, *frecv,
):
    e = lax.axis_index("hi") * n_lo + lax.axis_index("lo")
    bits = (n_hi * n_lo).bit_length() - 1
    lo_bits = n_lo.bit_length() - 1
    levels = [b for b in range(bits) if b != lo_bits - 1]
    depth = len(levels)
    boxes = 4

    def where_is(device):
        return (device // n_lo, device % n_lo)

    def flip(bit):
        return e + (1 - 2 * ((e // (1 << bit)) % 2)) * (1 << bit)

    dims = []
    for d in range(3):
        own_bits = [t - 2 for t in range(2, bits + 2) if t % 3 == d]
        coord = 0
        for place, bit in enumerate(own_bits):
            coord = coord + (e // (1 << bit)) % 2 * (1 << place)
        rest = e - spread(coord, own_bits)
        dims.append((own_bits, coord, rest, 1 << len(own_bits)))

    def at(d, coordinate):
        own_bits, _, rest, _ = dims[d]
        return rest + spread(coordinate, own_bits)

    (_, xc, _, nx), (_, yc, _, ny), (_, zc, _, nz) = dims
    par = zc % 2
    mate = 2 - 2 * par
    third = 2 * par
    z_to = zc + 2 - 4 * par
    z_from = zc - 2 + 4 * par
    z_sends = jnp.logical_and(z_to >= 0, z_to < nz)
    z_receives = jnp.logical_and(z_from >= 0, z_from < nz)

    barrier = pltpu.get_barrier_semaphore()

    def greet(device):
        pl.semaphore_signal(barrier, inc=1, device_id=where_is(device), device_id_type=MESH)

    for bit in levels:
        greet(flip(bit))
    others = []
    for d, n, c in ((0, nx, xc), (1, ny, yc)):
        others.append((c > 0, at(d, (c + n - 1) % n)))
        others.append((c < n - 1, at(d, (c + 1) % n)))
    others.append((z_sends, at(2, (z_to + nz) % nz)))
    others.append((z_receives, at(2, (z_from + nz) % nz)))
    for there, device in others:
        @pl.when(there)
        def _(device=device):
            greet(device)

    box_of = []
    rasters = [(cell_ref[j, 1] % 2) * 2 + cell_ref[j, 0] % 2 for j in range(boxes)]
    for s in range(boxes):
        found = 0
        for j in range(1, boxes):
            found = found + jnp.where(rasters[j] == s, j, 0)
        box_of.append(jnp.minimum(found, boxes - 1))

    rank = lin_ref.shape[1]
    for g in range(boxes):
        for ll, leaf in ((ll_in, lin_ref), (ll_out, lout_ref)):
            zero = jnp.zeros((rank, 128), BF)
            ll[g, 0:rank, 0:128] = leaf[g]
            ll[g, 0:rank, 128:256] = zero
            ll[g, rank : 2 * rank, 0:128] = zero
            ll[g, rank : 2 * rank, 128:256] = leaf[g]
        wbuf[g] = (contrast_ref[g : g + 1, :] * fields_ref[g].astype(F32)).astype(BF)
        w = wbuf[g]
        lhs = jnp.concatenate([w[0:32], w[32:64]], axis=1)
        fsend[0, g] = dot(lhs, ll_in[g], NT).astype(BF)

    row = lax.broadcasted_iota(jnp.int32, (16, 128), 0)
    for s in range(boxes):
        b = box_of[s]
        place = (1, 1 + s // 2, 1 + s % 2)
        grid[place + (slice(0, 64),)] = wbuf[b]
        grid[place + (slice(64, 128),)] = adj_ref[b]
        c = coords_ref[b].astype(F32) * 8.0
        cx, cy, cz = c[0:1], c[1:2], c[2:3]
        norm = cx * cx + cy * cy + cz * cz
        high = jnp.floor(norm * (1.0 / 256.0)) * 256.0
        low = norm - high
        one = jnp.ones_like(low)
        zero = jnp.zeros_like(low)

        def stack(rows):
            value = jnp.broadcast_to(zero, (16, 128))
            for k, r in enumerate(rows):
                value = jnp.where(row == k, r, value)
            return value.astype(BF)

        grid[place + (slice(128, 144),)] = stack([cx, cy, cz, high, low, one, one])
        tgt[s] = stack([-2.0 * cx, -2.0 * cy, -2.0 * cz, one, one, high, low])

    def build(i, _):
        l, g = i // boxes, i % boxes
        zero = jnp.zeros((rank, rank), BF)
        for part in range(2):
            m = mix_ref[l, g, part]
            base = part * 128
            blocks[l, g, 0:rank, base : base + 128] = jnp.concatenate([m, zero], axis=1)
            blocks[l, g, rank : 2 * rank, base : base + 128] = jnp.concatenate([zero, m], axis=1)
        return 0

    lax.fori_loop(0, depth * boxes, build, 0)

    def inverse(l, s):
        found = 0
        for j in range(1, boxes):
            found = found + jnp.where(perm_ref[l, j] == s, j, 0)
        return jnp.minimum(found, boxes - 1)

    def back_products(l, backs):
        own = []
        for g in range(boxes):
            both = dot(backs[g], blocks[l, g])
            own.append(both[:, 0:128])
            carry[l, g] = both[:, 128:256].astype(BF)
        for s in range(boxes):
            bsend[l, s] = carry[l, inverse(l, s)]
        return own

    backs = []
    for g in range(boxes):
        a = adj_ref[g]
        lhs = jnp.concatenate([a[0:32], a[32:64]], axis=1)
        backs.append(dot(lhs, ll_out[g], NT).astype(BF))
    own_terms = back_products(depth - 1, backs)
    acc[...] = jnp.zeros_like(acc)

    def remote(src, dst, sem, device):
        return pltpu.make_async_remote_copy(
            src_ref=src, dst_ref=dst, send_sem=send_sem.at[sem], recv_sem=recv_sem.at[sem],
            device_id=where_is(device), device_id_type=MESH,
        )

    def forward_copy(l):
        return remote(fsend.at[l], frecv[l], l, flip(levels[l]))

    def back_copy(l):
        return remote(bsend.at[l], brecv.at[l], depth + l, flip(levels[l]))

    first_sem = 2 * depth
    z1 = remote(
        grid.at[1, pl.ds(1, 2), pl.ds(1, 2)],
        grid.at[third, pl.ds(1, 2), pl.ds(1, 2)],
        first_sem, flip(0),
    )
    z2 = remote(
        grid.at[mate, pl.ds(1, 2), pl.ds(1, 2)],
        grid.at[third, pl.ds(1, 2), pl.ds(1, 2)],
        first_sem + 1, at(2, (z_to + nz) % nz),
    )

    def y_copies(plane, kind):
        sem = first_sem + 2 + 4 * kind
        up = remote(
            grid.at[plane, 2, pl.ds(1, 2)], grid.at[plane, 0, pl.ds(1, 2)],
            sem, at(1, (yc + 1) % ny),
        )
        down = remote(
            grid.at[plane, 1, pl.ds(1, 2)], grid.at[plane, 3, pl.ds(1, 2)],
            sem + 1, at(1, (yc + ny - 1) % ny),
        )
        return ((up, yc < ny - 1, yc > 0), (down, yc > 0, yc < ny - 1))

    def x_copies(plane, kind):
        sem = first_sem + 4 + 4 * kind
        up = remote(
            grid.at[plane, pl.ds(0, 4), 2], grid.at[plane, pl.ds(0, 4), 0],
            sem, at(0, (xc + 1) % nx),
        )
        down = remote(
            grid.at[plane, pl.ds(0, 4), 1], grid.at[plane, pl.ds(0, 4), 3],
            sem + 1, at(0, (xc + nx - 1) % nx),
        )
        return ((up, xc < nx - 1, xc > 0), (down, xc > 0, xc < nx - 1))

    def start(copies):
        for copy, sends, _ in copies:
            @pl.when(sends)
            def _(copy=copy):
                copy.start()

    def arrive(copies):
        for copy, _, receives in copies:
            @pl.when(receives)
            def _(copy=copy):
                copy.wait_recv()

    def sent(copies):
        for copy, sends, _ in copies:
            @pl.when(sends)
            def _(copy=copy):
                copy.wait_send()

    own_y, own_x = y_copies(1, 0), x_copies(1, 0)
    mate_y, mate_x = y_copies(mate, 1), x_copies(mate, 1)
    third_y, third_x = y_copies(third, 2), x_copies(third, 2)
    z2_copies = ((z2, z_sends, z_receives),)

    y_low, y_high = 1 - (yc + ny - 1) // ny, (yc + 1) // ny
    x_low, x_high = 1 - (xc + nx - 1) // nx, (xc + 1) // nx

    def clamp(v, low, high):
        return v + (1 - (v + 3) // 4) * low - (v // 3) * high

    def near(plane, first, last):
        def step(i, _):
            t, dy = i // 3, i % 3
            ty, tx = t // 2, t % 2
            y = clamp(ty + dy, y_low, y_high)
            goal = tgt[t]
            values, reals, imags = [], [], []
            for dx in range(3):
                x = clamp(tx + dx, x_low, x_high)
                values.append(grid[plane, y, x, 0:128])
                squared = dot(grid[plane, y, x, 128:144], goal, TN)
                real, imag = oscillation(squared, scale)
                reals.append(real)
                imags.append(imag)
            rhs = jnp.concatenate(
                [jnp.concatenate(reals, axis=0), jnp.concatenate(imags, axis=0)], axis=1
            )
            acc[t] = acc[t] + dot(jnp.concatenate(values, axis=1), rhs)
            return 0

        lax.fori_loop(first * 3, last * 3, step, 0)

    peers = depth
    for there, _ in others:
        peers = peers + there.astype(jnp.int32)
    pl.semaphore_wait(barrier, peers)

    forward_copy(0).start()
    back_copy(depth - 1).start()
    z1.start()
    start(own_y)

    coefs = [fsend[0, g] for g in range(boxes)]

    def step(i, coefs, own_terms):
        mine = [dot(coefs[g], blocks[i, g, :, 0:128], NT) for g in range(boxes)]
        forward_copy(i).wait_recv()
        new = []
        for g in range(boxes):
            arrived = frecv[i][perm_ref[i, g]]
            c = (mine[g] + dot(arrived, blocks[i, g, :, 128:256], NT)).astype(BF)
            new.append(c)
            if i + 1 < depth:
                fsend[i + 1, g] = c
        if i + 1 < depth:
            forward_copy(i + 1).start()
        l = depth - 1 - i
        back_copy(l).wait_recv()
        backs = [(own_terms[g] + brecv[l, g].astype(F32)).astype(BF) for g in range(boxes)]
        if l > 0:
            own_terms = back_products(l - 1, backs)
            back_copy(l - 1).start()
        return new, backs, own_terms

    def after(i):
        if i == 0:
            arrive(own_y)
            start(own_x)
        if i == 1:
            arrive(own_x)
            near(1, 0, 1)
        if i == 2:
            near(1, 1, 2)
        if i == 3:
            near(1, 2, 3)
        if i == 4:
            z1.wait_recv()
            start(z2_copies)
            start(mate_y)
            near(1, 3, 4)
        if i == 5:
            arrive(z2_copies)
            arrive(mate_y)

            @pl.when(z_receives)
            def _():
                start(third_y)

            start(mate_x)
        if i == 6:
            @pl.when(z_receives)
            def _():
                arrive(third_y)
                start(third_x)

            arrive(mate_x)
            near(mate, 0, 2)

    for i in range(depth):
        coefs, backs, own_terms = step(i, coefs, own_terms)
        after(i)
    for i in range(depth, 8):
        after(i)
    near(mate, 2, 4)

    @pl.when(z_receives)
    def _():
        arrive(third_x)

    near(third + (1 - third) * (1 - z_receives.astype(jnp.int32)), 0, 4)

    for g in range(boxes):
        a = acc[rasters[g]]
        ar, ai = a[:, 0:128], a[:, 128:256]
        far = dot(coefs[g], ll_out[g])
        out_ref[g, 0:32] = (
            fields_ref[g, 0:32].astype(F32) - (ar[0:32] - ai[32:64] + far[:, 0:128])
        ).astype(BF)
        out_ref[g, 32:64] = (
            fields_ref[g, 32:64].astype(F32) - (ai[0:32] + ar[32:64] + far[:, 128:256])
        ).astype(BF)
        far = dot(backs[g], ll_in[g])
        contrast = contrast_ref[g : g + 1, :]
        adj_out_ref[g, 0:32] = (
            adj_ref[g, 0:32].astype(F32) - contrast * (ar[64:96] + ai[96:128] + far[:, 0:128])
        ).astype(BF)
        adj_out_ref[g, 32:64] = (
            adj_ref[g, 32:64].astype(F32) - contrast * (ar[96:128] - ai[64:96] + far[:, 128:256])
        ).astype(BF)

    for l in range(depth):
        forward_copy(l).wait_send()
        back_copy(l).wait_send()
    z1.wait_send()
    sent(z2_copies)
    sent(own_y)
    sent(own_x)
    sent(mate_y)
    sent(mate_x)

    @pl.when(z_receives)
    def _():
        sent(third_y)
        sent(third_x)


def body(fields, adjoint_in, contrast, coords, neighbours, partner_perm, leaf_in, leaf_out, mixing):
    boxes, parts, sides, points = fields.shape
    depth = mixing.shape[0]
    rank = leaf_in.shape[1]
    n_hi, n_lo = lax.axis_size("hi"), lax.axis_size("lo")
    cells = jnp.floor(coords[:, 0:2, 0].astype(F32)).astype(jnp.int32)
    scale = 1.0 / math.sqrt(27 * points)
    vmem = pl.BlockSpec(memory_space=pltpu.VMEM)
    smem = pl.BlockSpec(memory_space=pltpu.SMEM)
    flat = (boxes, parts * sides, points)
    copies = 2 * depth + 14
    level = (depth, boxes, sides, 2 * rank)
    out = pl.pallas_call(
        functools.partial(kernel, n_hi, n_lo, scale),
        out_shape=[jax.ShapeDtypeStruct(flat, BF)] * 2,
        in_specs=[smem] * 2 + [vmem] * 7,
        out_specs=[vmem] * 2,
        scratch_shapes=[
            pltpu.VMEM((3, 4, 4, ROWS, points), BF),
            pltpu.VMEM((boxes, 16, points), BF),
            pltpu.VMEM((boxes, 4 * sides, 2 * points), F32),
            pltpu.VMEM(flat, BF),
            pltpu.VMEM((boxes, 2 * rank, 2 * points), BF),
            pltpu.VMEM((boxes, 2 * rank, 2 * points), BF),
            pltpu.VMEM((depth, boxes, 2 * rank, 4 * rank), BF),
            pltpu.VMEM(level, BF),
            pltpu.VMEM(level, BF),
            pltpu.VMEM(level, BF),
            pltpu.VMEM(level, BF),
            pltpu.SemaphoreType.DMA((copies,)),
            pltpu.SemaphoreType.DMA((copies,)),
        ]
        + [pltpu.VMEM(level[1:], BF)] * depth,
        compiler_params=pltpu.CompilerParams(
            collective_id=0, has_side_effects=True, vmem_limit_bytes=40 * 1024 * 1024
        ),
        name="operator",
    )(
        cells,
        partner_perm.reshape(depth, boxes),
        fields.reshape(flat),
        adjoint_in.reshape(flat),
        contrast,
        coords,
        leaf_in,
        leaf_out,
        mixing,
    )
    return (out[0].reshape(fields.shape), out[1].reshape(fields.shape))


def solution(mesh):
    split = ("hi", "lo")
    in_specs = (
        P(split, None, None, None),
        P(split, None, None, None),
        P(split, None),
        P(split, None, None),
        P(split, None),
        P(None, split, None),
        P(split, None, None),
        P(split, None, None),
        P(None, split, None, None, None),
    )
    out_specs = (P(split, None, None, None), P(split, None, None, None))
    return jax.shard_map(body, mesh=mesh, in_specs=in_specs, out_specs=out_specs, check_vma=False)
```

time: 684 us -> 103 us (0.15)
  the two profiles are of different devices: /device:TPU:25 before, /device:TPU:14 now
where the time goes in v1:
time: 103 us
  Pallas kernels  94 us (91%)
  local copies, waits for them, and re-layouts  7.88 us (8%)
    pallas_call x1, Pallas kernels, body(): pl.pallas_call(functools.partial(kernel, n_hi, n_lo, scale), out_shape=[j...  94 us
    unnamed x19, local copies, waits for them, and re-layouts  7.69 us

profile of v1, /device:TPU:14, one launch (start us, length us, event | category | flops | bytes accessed | tf_op | source)
XLA Modules:
  0.0 102.6 jit_solution(17149235124432097395)
XLA Ops:
  0.6 0.0 copy-start.7
  0.6 0.7 copy-done.7
  1.3 0.0 copy-start.6
  1.3 0.1 copy.14.perm_ref
  1.4 0.6 copy-done.6
  2.0 0.0 copy-start.5
  2.0 0.1 copy.16
  2.1 0.6 copy-done.5
  2.7 0.0 copy-start
  2.7 1.2 %copy-done = bf16[8,4,2,64,64]{4,3,2,1,0:T(8,128)(2,1)S(1)} copy-done((bf16[8,4,2,64,64]{4,3,2,1,0:T(8,128)(2,1)S(1)}, bf16[8,4,2,64,64]{4,3,2,1,0:T(8,128)(2,1)}, u32[]{:S(2)}) %copy-start) | copy-done | bytes 524312
  3.9 0.0 copy-start.1
  3.9 0.8 copy-done.1
  4.8 0.0 copy-start.2
  4.8 0.8 copy-done.2
  5.6 0.0 copy-start.3
  5.6 0.8 copy-done.3
  6.4 0.0 copy-start.4
  6.4 0.8 copy-done.4
  7.3 94.0 %operator.1 = (bf16[4,64,128]{2,1,0:T(8,128)(2,1)S(1)}, bf16[4,64,128]{2,1,0:T(8,128)(2,1)S(1)}) custom-call(s32[4,2]{1,0:T(4,128)S(1)} %bitcast.10, s32[8,4]{1,0:T(8,128)S(1)} %copy.14.perm_ref, bf16[4,64,128]{2,1,0:T(8,128)(2,1)S(1)} %bitcast.6, bf16[4,64,128]{2,1,0:T(8,128)(2,1)S(1)} %bitcast.7, f32[4,128]{1,0:T(4,128)S(1)} %copy-done.5, ...), custom_call_target="tpu_custom_call" | custom-call | tf_op jit(solution)/shard_map/operator/pallas_call | solution.py:431
  101.3 0.6 copy.19
  101.9 0.6 copy.20
  (2 shorter events, 0.0 us)
Async XLA Ops:
  0.6 0.7 copy-start.7
  1.3 0.7 copy-start.6
  2.0 0.7 copy-start.5
  2.7 1.2 %copy-start = (bf16[8,4,2,64,64]{4,3,2,1,0:T(8,128)(2,1)S(1)}, bf16[8,4,2,64,64]{4,3,2,1,0:T(8,128)(2,1)}, u32[]{:S(2)}) copy-start(bf16[8,4,2,64,64]{4,3,2,1,0:T(8,128)(2,1)} %mix_ref.1) | copy-start | bytes 1572868
  3.9 0.8 copy-start.1
  4.8 0.8 copy-start.2
  5.6 0.8 copy-start.3
  6.4 0.8 copy-start.4

commit v2 on v1

--- a/solution.py
+++ b/solution.py
@@ -65,11 +65,23 @@
 
 def kernel(
     n_hi, n_lo, scale,
-    cell_ref, perm_ref, fields_ref, adj_ref, contrast_ref, coords_ref, lin_ref, lout_ref, mix_ref,
-    out_ref, adj_out_ref,
-    grid, tgt, acc, wbuf, ll_in, ll_out, blocks, fsend, bsend, brecv, carry,
-    send_sem, recv_sem, *frecv,
+    perm_ref, coords_ref, *refs,
 ):
+    operands, refs = refs[:6], refs[6:]
+    out_ref, adj_out_ref, *refs = refs
+    (fields_ref, adj_ref, contrast_ref, lin_ref, lout_ref, mix_ref), refs = refs[:6], refs[6:]
+    (
+        grid, tgt, acc, ll_in, ll_out, blocks, fsend, bsend, brecv, carry, relays,
+        send_sem, recv_sem, load_sem, *frecv,
+    ) = refs
+    loads = [
+        pltpu.make_async_copy(src, dst, load_sem.at[i])
+        for i, (src, dst) in enumerate(
+            zip(operands, (fields_ref, adj_ref, contrast_ref, lin_ref, lout_ref, mix_ref))
+        )
+    ]
+    for load in loads:
+        load.start()
     e = lax.axis_index("hi") * n_lo + lax.axis_index("lo")
     bits = (n_hi * n_lo).bit_length() - 1
     lo_bits = n_lo.bit_length() - 1
@@ -105,6 +117,20 @@
     z_sends = jnp.logical_and(z_to >= 0, z_to < nz)
     z_receives = jnp.logical_and(z_from >= 0, z_from < nz)
 
+    ring_bits = list(range(lo_bits + 1, bits)) + [0]
+    ring = 1 << len(ring_bits)
+    zpos = 0
+    for place, bit in enumerate(ring_bits):
+        zpos = zpos + (e // (1 << bit)) % 2 * (1 << place)
+
+    def on_ring(shift):
+        return e - spread(zpos, ring_bits) + spread((zpos + ring + shift) % ring, ring_bits)
+
+    def side(shift):
+        return (zpos + ring + shift) % ring // (ring // 2)
+
+    far_hop = ring // 2 - 1
+
     barrier = pltpu.get_barrier_semaphore()
 
     def greet(device):
@@ -112,6 +138,8 @@
 
     for bit in levels:
         greet(flip(bit))
+    for shift in (far_hop, -far_hop, 1, -1):
+        greet(on_ring(shift))
     others = []
     for d, n, c in ((0, nx, xc), (1, ny, yc)):
         others.append((c > 0, at(d, (c + n - 1) % n)))
@@ -123,15 +151,44 @@
         def _(device=device):
             greet(device)
 
-    box_of = []
-    rasters = [(cell_ref[j, 1] % 2) * 2 + cell_ref[j, 0] % 2 for j in range(boxes)]
+    rank = lin_ref.shape[1]
+    c = coords_ref[...].astype(F32)
+    cells = jnp.floor(c)
+    odd = cells - 2.0 * jnp.floor(0.5 * cells)
+    raster = odd[0] + 2.0 * odd[1]
+    c = c * 8.0
+    norm = c[0] * c[0] + c[1] * c[1] + c[2] * c[2]
+    high = jnp.floor(norm * (1.0 / 256.0)) * 256.0
+    low = norm - high
+
+    def holds(g, s):
+        return raster[g : g + 1] == float(s)
+
+    def pick(s, values):
+        total = values[0]
+        for g in range(1, boxes):
+            total = jnp.where(holds(g, s), values[g], total)
+        return total
+
+    row = lax.broadcasted_iota(jnp.int32, (16, 128), 0)
+
+    def stack(rows):
+        value = jnp.zeros((16, 128), F32)
+        for k, r in enumerate(rows):
+            value = jnp.where(row == k, r, value)
+        return value.astype(BF)
+
+    one = jnp.ones((1, 128), F32)
     for s in range(boxes):
-        found = 0
-        for j in range(1, boxes):
-            found = found + jnp.where(rasters[j] == s, j, 0)
-        box_of.append(jnp.minimum(found, boxes - 1))
-
-    rank = lin_ref.shape[1]
+        x, y, z, h, w = (
+            pick(s, [v[g : g + 1] for g in range(boxes)]) for v in (c[0], c[1], c[2], high, low)
+        )
+        grid[1, 1 + s // 2, 1 + s % 2, 128:144] = stack([x, y, z, h, w, one, one])
+        tgt[s] = stack([-2.0 * x, -2.0 * y, -2.0 * z, one, one, h, w])
+
+    for load in loads[:5]:
+        load.wait()
+    weighted = []
     for g in range(boxes):
         for ll, leaf in ((ll_in, lin_ref), (ll_out, lout_ref)):
             zero = jnp.zeros((rank, 128), BF)
@@ -139,33 +196,18 @@
             ll[g, 0:rank, 128:256] = zero
             ll[g, rank : 2 * rank, 0:128] = zero
             ll[g, rank : 2 * rank, 128:256] = leaf[g]
-        wbuf[g] = (contrast_ref[g : g + 1, :] * fields_ref[g].astype(F32)).astype(BF)
-        w = wbuf[g]
-        lhs = jnp.concatenate([w[0:32], w[32:64]], axis=1)
+        w = contrast_ref[g : g + 1, :] * fields_ref[g].astype(F32)
+        weighted.append(w)
+        lhs = jnp.concatenate([w[0:32], w[32:64]], axis=1).astype(BF)
         fsend[0, g] = dot(lhs, ll_in[g], NT).astype(BF)
-
-    row = lax.broadcasted_iota(jnp.int32, (16, 128), 0)
     for s in range(boxes):
-        b = box_of[s]
         place = (1, 1 + s // 2, 1 + s % 2)
-        grid[place + (slice(0, 64),)] = wbuf[b]
-        grid[place + (slice(64, 128),)] = adj_ref[b]
-        c = coords_ref[b].astype(F32) * 8.0
-        cx, cy, cz = c[0:1], c[1:2], c[2:3]
-        norm = cx * cx + cy * cy + cz * cz
-        high = jnp.floor(norm * (1.0 / 256.0)) * 256.0
-        low = norm - high
-        one = jnp.ones_like(low)
-        zero = jnp.zeros_like(low)
-
-        def stack(rows):
-            value = jnp.broadcast_to(zero, (16, 128))
-            for k, r in enumerate(rows):
-                value = jnp.where(row == k, r, value)
-            return value.astype(BF)
-
-        grid[place + (slice(128, 144),)] = stack([cx, cy, cz, high, low, one, one])
-        tgt[s] = stack([-2.0 * cx, -2.0 * cy, -2.0 * cz, one, one, high, low])
+        grid[place + (slice(0, 64),)] = pick(s, weighted).astype(BF)
+        grid[place + (slice(64, 128),)] = pick(
+            s, [adj_ref[g].astype(F32) for g in range(boxes)]
+        ).astype(BF)
+
+    loads[5].wait()
 
     def build(i, _):
         l, g = i // boxes, i % boxes
@@ -182,7 +224,7 @@
     def inverse(l, s):
         found = 0
         for j in range(1, boxes):
-            found = found + jnp.where(perm_ref[l, j] == s, j, 0)
+            found = found + jnp.where(perm_ref[j, l] == s, j, 0)
         return jnp.minimum(found, boxes - 1)
 
     def back_products(l, backs):
@@ -216,10 +258,18 @@
         return remote(bsend.at[l], brecv.at[l], depth + l, flip(levels[l]))
 
     first_sem = 2 * depth
-    z1 = remote(
-        grid.at[1, pl.ds(1, 2), pl.ds(1, 2)],
-        grid.at[third, pl.ds(1, 2), pl.ds(1, 2)],
-        first_sem, flip(0),
+    last_sem = first_sem + 14
+    up_first = remote(
+        grid.at[1, 1, pl.ds(1, 2)], relays.at[0], first_sem, on_ring(far_hop)
+    )
+    down_first = remote(
+        grid.at[1, 2, pl.ds(1, 2)], relays.at[1], last_sem, on_ring(-far_hop)
+    )
+    up_last = remote(
+        relays.at[0], grid.at[2 * side(-far_hop), 1, pl.ds(1, 2)], last_sem + 1, on_ring(1)
+    )
+    down_last = remote(
+        relays.at[1], grid.at[2 * side(far_hop), 2, pl.ds(1, 2)], last_sem + 2, on_ring(-1)
     )
     z2 = remote(
         grid.at[mate, pl.ds(1, 2), pl.ds(1, 2)],
@@ -302,14 +352,15 @@
 
         lax.fori_loop(first * 3, last * 3, step, 0)
 
-    peers = depth
+    peers = depth + 4
     for there, _ in others:
         peers = peers + there.astype(jnp.int32)
     pl.semaphore_wait(barrier, peers)
 
     forward_copy(0).start()
     back_copy(depth - 1).start()
-    z1.start()
+    up_first.start()
+    down_first.start()
     start(own_y)
 
     coefs = [fsend[0, g] for g in range(boxes)]
@@ -319,7 +370,7 @@
         forward_copy(i).wait_recv()
         new = []
         for g in range(boxes):
-            arrived = frecv[i][perm_ref[i, g]]
+            arrived = frecv[i][perm_ref[g, i]]
             c = (mine[g] + dot(arrived, blocks[i, g, :, 128:256], NT)).astype(BF)
             new.append(c)
             if i + 1 < depth:
@@ -339,32 +390,36 @@
             arrive(own_y)
             start(own_x)
         if i == 1:
+            up_first.wait_recv()
+            up_last.start()
+            down_first.wait_recv()
+            down_last.start()
+        if i == 2:
             arrive(own_x)
             near(1, 0, 1)
-        if i == 2:
-            near(1, 1, 2)
-        if i == 3:
-            near(1, 2, 3)
-        if i == 4:
-            z1.wait_recv()
+            up_last.wait_recv()
+            down_last.wait_recv()
             start(z2_copies)
             start(mate_y)
-            near(1, 3, 4)
-        if i == 5:
+        if i == 3:
+            near(1, 1, 2)
+            arrive(mate_y)
+            start(mate_x)
             arrive(z2_copies)
-            arrive(mate_y)
 
             @pl.when(z_receives)
             def _():
                 start(third_y)
-
-            start(mate_x)
-        if i == 6:
+        if i == 4:
+            near(1, 2, 3)
+
             @pl.when(z_receives)
             def _():
                 arrive(third_y)
                 start(third_x)
-
+        if i == 5:
+            near(1, 3, 4)
+        if i == 6:
             arrive(mate_x)
             near(mate, 0, 2)
 
@@ -382,7 +437,10 @@
     near(third + (1 - third) * (1 - z_receives.astype(jnp.int32)), 0, 4)
 
     for g in range(boxes):
-        a = acc[rasters[g]]
+        a = acc[0]
+        for s in range(1, boxes):
+            inside = jnp.concatenate([holds(g, s), holds(g, s)], axis=1)
+            a = jnp.where(inside, acc[s], a)
         ar, ai = a[:, 0:128], a[:, 128:256]
         far = dot(coefs[g], ll_out[g])
         out_ref[g, 0:32] = (
@@ -403,7 +461,10 @@
     for l in range(depth):
         forward_copy(l).wait_send()
         back_copy(l).wait_send()
-    z1.wait_send()
+    up_first.wait_send()
+    down_first.wait_send()
+    up_last.wait_send()
+    down_last.wait_send()
     sent(z2_copies)
     sent(own_y)
     sent(own_x)
@@ -421,23 +482,26 @@
     depth = mixing.shape[0]
     rank = leaf_in.shape[1]
     n_hi, n_lo = lax.axis_size("hi"), lax.axis_size("lo")
-    cells = jnp.floor(coords[:, 0:2, 0].astype(F32)).astype(jnp.int32)
     scale = 1.0 / math.sqrt(27 * points)
     vmem = pl.BlockSpec(memory_space=pltpu.VMEM)
     smem = pl.BlockSpec(memory_space=pltpu.SMEM)
+    away = pl.BlockSpec(memory_space=pl.ANY)
     flat = (boxes, parts * sides, points)
-    copies = 2 * depth + 14
+    copies = 2 * depth + 17
     level = (depth, boxes, sides, 2 * rank)
+    inputs = (
+        fields.reshape(flat), adjoint_in.reshape(flat), contrast, leaf_in, leaf_out, mixing,
+    )
     out = pl.pallas_call(
         functools.partial(kernel, n_hi, n_lo, scale),
         out_shape=[jax.ShapeDtypeStruct(flat, BF)] * 2,
-        in_specs=[smem] * 2 + [vmem] * 7,
+        in_specs=[smem, vmem] + [away] * 6,
         out_specs=[vmem] * 2,
-        scratch_shapes=[
+        scratch_shapes=[pltpu.VMEM(v.shape, v.dtype) for v in inputs]
+        + [
             pltpu.VMEM((3, 4, 4, ROWS, points), BF),
             pltpu.VMEM((boxes, 16, points), BF),
             pltpu.VMEM((boxes, 4 * sides, 2 * points), F32),
-            pltpu.VMEM(flat, BF),
             pltpu.VMEM((boxes, 2 * rank, 2 * points), BF),
             pltpu.VMEM((boxes, 2 * rank, 2 * points), BF),
             pltpu.VMEM((depth, boxes, 2 * rank, 4 * rank), BF),
@@ -445,24 +509,20 @@
             pltpu.VMEM(level, BF),
             pltpu.VMEM(level, BF),
             pltpu.VMEM(level, BF),
+            pltpu.VMEM((2, 2, ROWS, points), BF),
             pltpu.SemaphoreType.DMA((copies,)),
             pltpu.SemaphoreType.DMA((copies,)),
+            pltpu.SemaphoreType.DMA((6,)),
         ]
         + [pltpu.VMEM(level[1:], BF)] * depth,
         compiler_params=pltpu.CompilerParams(
-            collective_id=0, has_side_effects=True, vmem_limit_bytes=40 * 1024 * 1024
+            collective_id=0, has_side_effects=True, vmem_limit_bytes=60 * 1024 * 1024
         ),
         name="operator",
     )(
-        cells,
-        partner_perm.reshape(depth, boxes),
-        fields.reshape(flat),
-        adjoint_in.reshape(flat),
-        contrast,
-        coords,
-        leaf_in,
-        leaf_out,
-        mixing,
+        partner_perm.reshape(depth, boxes).T,
+        coords.swapaxes(0, 1),
+        *inputs,
     )
     return (out[0].reshape(fields.shape), out[1].reshape(fields.shape))
 

time: 103 us -> 100 us (0.971)
  the two profiles are of different devices: /device:TPU:14 before, /device:TPU:16 now
where the time goes in v2:
time: 100 us
  Pallas kernels  97.3 us (97%)
  local copies, waits for them, and re-layouts  2.14 us (2%)
    pallas_call x1, Pallas kernels, body(): pl.pallas_call(functools.partial(kernel, n_hi, n_lo, scale), out_shape=[j...  97.3 us
    unnamed x4, local copies, waits for them, and re-layouts  2.14 us

profile of v2, /device:TPU:16, one launch (start us, length us, event | category | flops | bytes accessed | tf_op | source)
XLA Modules:
  0.0 100.1 jit_solution(4109855949601568033)
XLA Ops:
  0.6 97.3 %operator.1 = (bf16[4,64,128]{2,1,0:T(8,128)(2,1)}, bf16[4,64,128]{2,1,0:T(8,128)(2,1)}) custom-call(s32[4,8]{1,0:T(4,128)} %bitcast.13, bf16[3,4,128]{2,1,0:T(4,128)(2,1)} %bitcast.12, bf16[4,64,128]{2,1,0:T(8,128)(2,1)} %bitcast.8, bf16[4,64,128]{2,1,0:T(8,128)(2,1)} %bitcast.9, f32[4,128]{1,0:T(4,128)} %refs_2_.1, bf16[4,64,128]{2,1,0:T(8,128)(2,1)} %refs_3_.1, ...), custom_call_target="tpu_custom_call" | custom-call | tf_op jit(solution)/shard_map/operator/pallas_call | solution.py:495
  98.0 0.0 copy-start
  98.0 1.5 %copy.12 = bf16[4,2,32,128]{3,2,1,0:T(8,128)(2,1)} copy(bf16[4,2,32,128]{3,2,1,0:T(8,128)(2,1)} %bitcast.11) | data formatting | bytes 131072
  99.5 0.0 copy-done
  99.5 0.6 copy.13
Async XLA Ops:
  98.0 1.5 %copy-start = (bf16[4,64,128]{2,1,0:T(8,128)(2,1)S(1)}, bf16[4,64,128]{2,1,0:T(8,128)(2,1)}, u32[]{:S(2)}) copy-start(bf16[4,64,128]{2,1,0:T(8,128)(2,1)} %get-tuple-element.5) | copy-start | bytes 196612

commit v3 on v2

--- a/solution.py
+++ b/solution.py
@@ -18,6 +18,14 @@
 F32 = jnp.float32
 NT = (((1,), (1,)), ((), ()))
 TN = (((0,), (0,)), ((), ()))
+
+
+ORDER = (
+    "SF", "SZ1", "SB", "F0", "SYo", "B0", "F1", "RYo", "SXo", "RD", "RU", "B1", "F2", "NAo1",
+    "NAo0", "B2", "Z", "SYm", "SZ2", "NAo2", "F3", "NAo3", "RYm", "SXm", "RZ2", "RXo", "SYt", "F4",
+    "B3", "NAm0", "NAm1", "B4", "NEo", "F5", "NEm", "RYt", "NEt", "ES", "B5", "NAt2", "NAm2", "RXm",
+    "F6", "NAt1", "B6", "SXt", "NAt3", "NAt0", "NAm3", "NCo", "NCm", "F7", "RXt", "NCt", "B7", "ER",
+)
 
 
 def fit(function, degree):
@@ -71,7 +79,7 @@
     out_ref, adj_out_ref, *refs = refs
     (fields_ref, adj_ref, contrast_ref, lin_ref, lout_ref, mix_ref), refs = refs[:6], refs[6:]
     (
-        grid, tgt, acc, ll_in, ll_out, blocks, fsend, bsend, brecv, carry, relays,
+        grid, tgt, acc, ll_in, ll_out, blocks, fsend, bsend, brecv, carry, relays, res, exsend, exrecv,
         send_sem, recv_sem, load_sem, *frecv,
     ) = refs
     loads = [
@@ -116,6 +124,15 @@
     z_from = zc - 2 + 4 * par
     z_sends = jnp.logical_and(z_to >= 0, z_to < nz)
     z_receives = jnp.logical_and(z_from >= 0, z_from < nz)
+
+    mirror = e // n_lo % 2
+    xm = xc + mirror * (nx - 1 - 2 * xc)
+    x_from, x_to = xc + 1 - 2 * mirror, xc - 1 + 2 * mirror
+    imports, exports = xm < nx - 1, xm > 0
+    far_edge, near_edge = (xm + 1) // nx, 1 - (xm + nx - 1) // nx
+
+    def column(v):
+        return v + mirror * (3 - 2 * v)
 
     ring_bits = list(range(lo_bits + 1, bits)) + [0]
     ring = 1 << len(ring_bits)
@@ -184,7 +201,9 @@
             pick(s, [v[g : g + 1] for g in range(boxes)]) for v in (c[0], c[1], c[2], high, low)
         )
         grid[1, 1 + s // 2, 1 + s % 2, 128:144] = stack([x, y, z, h, w, one, one])
-        tgt[s] = stack([-2.0 * x, -2.0 * y, -2.0 * z, one, one, h, w])
+        tgt[s // 2 * 3 + column(1 + s % 2) - 1] = stack(
+            [-2.0 * x, -2.0 * y, -2.0 * z, one, one, h, w]
+        )
 
     for load in loads[:5]:
         load.wait()
@@ -290,16 +309,14 @@
         return ((up, yc < ny - 1, yc > 0), (down, yc > 0, yc < ny - 1))
 
     def x_copies(plane, kind):
-        sem = first_sem + 4 + 4 * kind
-        up = remote(
-            grid.at[plane, pl.ds(0, 4), 2], grid.at[plane, pl.ds(0, 4), 0],
-            sem, at(0, (xc + 1) % nx),
-        )
-        down = remote(
-            grid.at[plane, pl.ds(0, 4), 1], grid.at[plane, pl.ds(0, 4), 3],
-            sem + 1, at(0, (xc + nx - 1) % nx),
-        )
-        return ((up, xc < nx - 1, xc > 0), (down, xc > 0, xc < nx - 1))
+        copy = remote(
+            grid.at[plane, pl.ds(0, 4), 1 + mirror], grid.at[plane, pl.ds(0, 4), 3 - 3 * mirror],
+            first_sem + 4 + 4 * kind, at(0, (x_to + nx) % nx),
+        )
+        return ((copy, exports, imports),)
+
+    extra = remote(exsend, exrecv, first_sem + 5, at(0, (x_from + nx) % nx))
+    extra_copies = ((extra, imports, exports),)
 
     def start(copies):
         for copy, sends, _ in copies:
@@ -325,47 +342,79 @@
     z2_copies = ((z2, z_sends, z_receives),)
 
     y_low, y_high = 1 - (yc + ny - 1) // ny, (yc + 1) // ny
-    x_low, x_high = 1 - (xc + nx - 1) // nx, (xc + 1) // nx
-
-    def clamp(v, low, high):
-        return v + (1 - (v + 3) // 4) * low - (v // 3) * high
-
-    def near(plane, first, last):
+    third_or_own = jnp.where(z_receives, third, 1)
+    rows_of = [y_low, 1, 2, 3 - y_high]
+
+    def near(first, stride, count):
         def step(i, _):
-            t, dy = i // 3, i % 3
-            ty, tx = t // 2, t % 2
-            y = clamp(ty + dy, y_low, y_high)
-            goal = tgt[t]
-            values, reals, imags = [], [], []
-            for dx in range(3):
-                x = clamp(tx + dx, x_low, x_high)
-                values.append(grid[plane, y, x, 0:128])
-                squared = dot(grid[plane, y, x, 128:144], goal, TN)
-                real, imag = oscillation(squared, scale)
-                reals.append(real)
-                imags.append(imag)
-            rhs = jnp.concatenate(
-                [jnp.concatenate(reals, axis=0), jnp.concatenate(imags, axis=0)], axis=1
+            j = first + stride * i
+            k, c = j // 6, j % 6
+            plane = 1 + k % 2 * (mate - 1) + k // 2 * (third_or_own - 1)
+            goal = (c + 4) // 6 + c // 5
+            source = 1 + c % 2 + 2 * (c // 4) - 2 * (c // 5)
+            x = column(source - far_edge * (c // 4 - c // 5))
+            weight = (1 + near_edge * (1 - (c + 4) // 5)).astype(F32)
+            for ty in range(2):
+                target = tgt[3 * ty + goal]
+                values, reals, imags = [], [], []
+                for dy in range(3):
+                    y = rows_of[ty + dy]
+                    values.append(grid[plane, y, x, 0:128])
+                    squared = dot(grid[plane, y, x, 128:144], target, TN)
+                    real, imag = oscillation(squared, scale)
+                    reals.append(real)
+                    imags.append(imag)
+                rhs = jnp.concatenate(
+                    [jnp.concatenate(reals, axis=0), jnp.concatenate(imags, axis=0)], axis=1
+                )
+                product = dot(jnp.concatenate(values, axis=1), rhs)
+                acc[3 * ty + goal] = acc[3 * ty + goal] + weight * product
+            return 0
+
+        lax.fori_loop(0, count, step, 0)
+
+    def combine(a):
+        ar, ai = a[:, 0:128], a[:, 128:256]
+        return jnp.concatenate(
+            [
+                ar[0:32] - ai[32:64], ai[0:32] + ar[32:64],
+                ar[64:96] + ai[96:128], ar[96:128] - ai[64:96],
+            ],
+            axis=0,
+        )
+
+    def neighbour_targets():
+        for ty in range(2):
+            f = grid[1, 1 + ty, 3 - 3 * mirror, 128:144].astype(F32)
+            tgt[3 * ty + 2] = stack(
+                [-2.0 * f[0:1], -2.0 * f[1:2], -2.0 * f[2:3], one, one, f[3:4], f[4:5]]
             )
-            acc[t] = acc[t] + dot(jnp.concatenate(values, axis=1), rhs)
-            return 0
-
-        lax.fori_loop(first * 3, last * 3, step, 0)
+
+    def send_extra():
+        for ty in range(2):
+            exsend[ty] = combine(acc[3 * ty + 2]).astype(BF)
+        start(extra_copies)
+
+    def receive_extra():
+        for ty in range(2):
+            for x in range(2):
+                res[2 * ty + x] = combine(acc[3 * ty + column(1 + x) - 1])
+
+        @pl.when(exports)
+        def _():
+            extra.wait_recv()
+            for ty in range(2):
+                mine = 2 * ty + mirror
+                res[mine] = res[mine] + exrecv[ty].astype(F32)
 
     peers = depth + 4
     for there, _ in others:
         peers = peers + there.astype(jnp.int32)
     pl.semaphore_wait(barrier, peers)
 
-    forward_copy(0).start()
-    back_copy(depth - 1).start()
-    up_first.start()
-    down_first.start()
-    start(own_y)
-
     coefs = [fsend[0, g] for g in range(boxes)]
 
-    def step(i, coefs, own_terms):
+    def forward_step(i, coefs):
         mine = [dot(coefs[g], blocks[i, g, :, 0:128], NT) for g in range(boxes)]
         forward_copy(i).wait_recv()
         new = []
@@ -377,85 +426,99 @@
                 fsend[i + 1, g] = c
         if i + 1 < depth:
             forward_copy(i + 1).start()
+        return new
+
+    def back_step(i, own_terms):
         l = depth - 1 - i
         back_copy(l).wait_recv()
         backs = [(own_terms[g] + brecv[l, g].astype(F32)).astype(BF) for g in range(boxes)]
         if l > 0:
             own_terms = back_products(l - 1, backs)
             back_copy(l - 1).start()
-        return new, backs, own_terms
-
-    def after(i):
-        if i == 0:
-            arrive(own_y)
-            start(own_x)
-        if i == 1:
-            up_first.wait_recv()
-            up_last.start()
-            down_first.wait_recv()
-            down_last.start()
-        if i == 2:
-            arrive(own_x)
-            near(1, 0, 1)
-            up_last.wait_recv()
-            down_last.wait_recv()
-            start(z2_copies)
-            start(mate_y)
-        if i == 3:
-            near(1, 1, 2)
-            arrive(mate_y)
-            start(mate_x)
-            arrive(z2_copies)
-
-            @pl.when(z_receives)
-            def _():
-                start(third_y)
-        if i == 4:
-            near(1, 2, 3)
-
-            @pl.when(z_receives)
-            def _():
-                arrive(third_y)
-                start(third_x)
-        if i == 5:
-            near(1, 3, 4)
-        if i == 6:
-            arrive(mate_x)
-            near(mate, 0, 2)
-
-    for i in range(depth):
-        coefs, backs, own_terms = step(i, coefs, own_terms)
-        after(i)
-    for i in range(depth, 8):
-        after(i)
-    near(mate, 2, 4)
-
-    @pl.when(z_receives)
-    def _():
-        arrive(third_x)
-
-    near(third + (1 - third) * (1 - z_receives.astype(jnp.int32)), 0, 4)
+        return backs, own_terms
+
+    def when_third(action, *copies):
+        @pl.when(z_receives)
+        def _():
+            for c in copies:
+                action(c)
+
+    def z_last():
+        up_last.wait_recv()
+        down_last.wait_recv()
+
+    def relay(first, last):
+        first.wait_recv()
+        last.start()
+
+    def own_columns():
+        arrive(own_x)
+        neighbour_targets()
+
+    actions = {
+        "SF": lambda: forward_copy(0).start(),
+        "SB": lambda: back_copy(depth - 1).start(),
+        "SYo": lambda: start(own_y), "RYo": lambda: arrive(own_y),
+        "SXo": lambda: start(own_x), "RXo": own_columns,
+        "SZ1": lambda: (up_first.start(), down_first.start()),
+        "RU": lambda: relay(up_first, up_last), "RD": lambda: relay(down_first, down_last),
+        "Z": z_last,
+        "SYm": lambda: start(mate_y), "RYm": lambda: arrive(mate_y),
+        "SXm": lambda: start(mate_x), "RXm": lambda: arrive(mate_x),
+        "SZ2": lambda: start(z2_copies), "RZ2": lambda: arrive(z2_copies),
+        "SYt": lambda: when_third(start, third_y), "RYt": lambda: when_third(arrive, third_y),
+        "SXt": lambda: when_third(start, third_x), "RXt": lambda: when_third(arrive, third_x),
+        "ES": send_extra, "ER": receive_extra,
+    }
+    pending = []
+
+    def run_near():
+        while pending:
+            stride = pending[1] - pending[0] if len(pending) > 1 else 1
+            count = 1
+            while count < len(pending) and pending[count] - pending[count - 1] == stride:
+                count += 1
+            near(pending[0], stride, count)
+            del pending[:count]
+
+    for word in ORDER:
+        if word[0] == "N":
+            c = {"A": int(word[-1]) if word[-1].isdigit() else 0, "C": 4, "E": 5}[word[1]]
+            pending.append("omt".index(word[2]) * 6 + c)
+            continue
+        run_near()
+        if word[0] == "F":
+            if int(word[1]) < depth:
+                coefs = forward_step(int(word[1]), coefs)
+        elif word[0] == "B":
+            if int(word[1]) < depth:
+                backs, own_terms = back_step(int(word[1]), own_terms)
+        else:
+            actions[word]()
+    run_near()
+
+    def pick_raster(g):
+        total = res[0]
+        for s in range(1, boxes):
+            total = jnp.where(holds(g, s), res[s], total)
+        return total
 
     for g in range(boxes):
-        a = acc[0]
-        for s in range(1, boxes):
-            inside = jnp.concatenate([holds(g, s), holds(g, s)], axis=1)
-            a = jnp.where(inside, acc[s], a)
-        ar, ai = a[:, 0:128], a[:, 128:256]
+        sums = pick_raster(g)
         far = dot(coefs[g], ll_out[g])
         out_ref[g, 0:32] = (
-            fields_ref[g, 0:32].astype(F32) - (ar[0:32] - ai[32:64] + far[:, 0:128])
+            fields_ref[g, 0:32].astype(F32) - (sums[0:32] + far[:, 0:128])
         ).astype(BF)
         out_ref[g, 32:64] = (
-            fields_ref[g, 32:64].astype(F32) - (ai[0:32] + ar[32:64] + far[:, 128:256])
+            fields_ref[g, 32:64].astype(F32) - (sums[32:64] + far[:, 128:256])
         ).astype(BF)
         far = dot(backs[g], ll_in[g])
         contrast = contrast_ref[g : g + 1, :]
         adj_out_ref[g, 0:32] = (
-            adj_ref[g, 0:32].astype(F32) - contrast * (ar[64:96] + ai[96:128] + far[:, 0:128])
+            adj_ref[g, 0:32].astype(F32) - contrast * (sums[64:96] + far[:, 0:128])
         ).astype(BF)
         adj_out_ref[g, 32:64] = (
-            adj_ref[g, 32:64].astype(F32) - contrast * (ar[96:128] - ai[64:96] + far[:, 128:256])
+            adj_ref[g, 32:64].astype(F32) - contrast * (sums[96:128] + far[:, 128:256])
         ).astype(BF)
 
     for l in range(depth):
@@ -470,6 +533,7 @@
     sent(own_x)
     sent(mate_y)
     sent(mate_x)
+    sent(extra_copies)
 
     @pl.when(z_receives)
     def _():
@@ -500,8 +564,8 @@
         scratch_shapes=[pltpu.VMEM(v.shape, v.dtype) for v in inputs]
         + [
             pltpu.VMEM((3, 4, 4, ROWS, points), BF),
-            pltpu.VMEM((boxes, 16, points), BF),
-            pltpu.VMEM((boxes, 4 * sides, 2 * points), F32),
+            pltpu.VMEM((6, 16, points), BF),
+            pltpu.VMEM((6, 4 * sides, 2 * points), F32),
             pltpu.VMEM((boxes, 2 * rank, 2 * points), BF),
             pltpu.VMEM((boxes, 2 * rank, 2 * points), BF),
             pltpu.VMEM((depth, boxes, 2 * rank, 4 * rank), BF),
@@ -510,6 +574,9 @@
             pltpu.VMEM(level, BF),
             pltpu.VMEM(level, BF),
             pltpu.VMEM((2, 2, ROWS, points), BF),
+            pltpu.VMEM((boxes, 4 * sides, points), F32),
+            pltpu.VMEM((2, 4 * sides, points), BF),
+            pltpu.VMEM((2, 4 * sides, points), BF),
             pltpu.SemaphoreType.DMA((copies,)),
             pltpu.SemaphoreType.DMA((copies,)),
             pltpu.SemaphoreType.DMA((6,)),

time: 100 us -> 77.5 us (0.78)
  the two profiles are of different devices: /device:TPU:16 before, /device:TPU:30 now
where the time goes in v3:
time: 77.5 us; the launch traced here: 77.3 us
  Pallas kernels  74.5 us (96%)
  local copies, waits for them, and re-layouts  2.14 us (3%)
    pallas_call x1, Pallas kernels, body(): pl.pallas_call(functools.partial(kernel, n_hi, n_lo, scale), out_shape=[j...  74.5 us
    unnamed x4, local copies, waits for them, and re-layouts  2.14 us

profile of v3, /device:TPU:30, one launch (start us, length us, event | category | flops | bytes accessed | tf_op | source)
XLA Modules:
  0.0 77.3 jit_solution(12306031098200951908)
XLA Ops:
  0.6 74.5 %operator.1 = (bf16[4,64,128]{2,1,0:T(8,128)(2,1)}, bf16[4,64,128]{2,1,0:T(8,128)(2,1)}) custom-call(s32[4,8]{1,0:T(4,128)} %bitcast.13, bf16[3,4,128]{2,1,0:T(4,128)(2,1)} %bitcast.12, bf16[4,64,128]{2,1,0:T(8,128)(2,1)} %bitcast.8, bf16[4,64,128]{2,1,0:T(8,128)(2,1)} %bitcast.9, f32[4,128]{1,0:T(4,128)} %refs_2_.1, bf16[4,64,128]{2,1,0:T(8,128)(2,1)} %refs_3_.1, ...), custom_call_target="tpu_custom_call" | custom-call | tf_op jit(solution)/shard_map/operator/pallas_call | solution.py:559
  75.2 0.0 copy-start
  75.2 1.5 %copy.12 = bf16[4,2,32,128]{3,2,1,0:T(8,128)(2,1)} copy(bf16[4,2,32,128]{3,2,1,0:T(8,128)(2,1)} %bitcast.11) | data formatting | bytes 131072
  76.7 0.0 copy-done
  76.7 0.6 copy.13
Async XLA Ops:
  75.2 1.5 %copy-start = (bf16[4,64,128]{2,1,0:T(8,128)(2,1)S(1)}, bf16[4,64,128]{2,1,0:T(8,128)(2,1)}, u32[]{:S(2)}) copy-start(bf16[4,64,128]{2,1,0:T(8,128)(2,1)} %get-tuple-element.5) | copy-start | bytes 196612

commit v4 on v3

--- a/solution.py
+++ b/solution.py
@@ -201,20 +201,22 @@
             pick(s, [v[g : g + 1] for g in range(boxes)]) for v in (c[0], c[1], c[2], high, low)
         )
         grid[1, 1 + s // 2, 1 + s % 2, 128:144] = stack([x, y, z, h, w, one, one])
-        tgt[s // 2 * 3 + column(1 + s % 2) - 1] = stack(
+        tgt[column(1 + s % 2) - 1, :, 128 * (s // 2) : 128 * (s // 2) + 128] = stack(
             [-2.0 * x, -2.0 * y, -2.0 * z, one, one, h, w]
         )
 
-    for load in loads[:5]:
+    def double(ll, leaf, g):
+        zero = jnp.zeros((rank, 128), BF)
+        ll[g, 0:rank, 0:128] = leaf[g]
+        ll[g, 0:rank, 128:256] = zero
+        ll[g, rank : 2 * rank, 0:128] = zero
+        ll[g, rank : 2 * rank, 128:256] = leaf[g]
+
+    for load in loads[:4]:
         load.wait()
     weighted = []
     for g in range(boxes):
-        for ll, leaf in ((ll_in, lin_ref), (ll_out, lout_ref)):
-            zero = jnp.zeros((rank, 128), BF)
-            ll[g, 0:rank, 0:128] = leaf[g]
-            ll[g, 0:rank, 128:256] = zero
-            ll[g, rank : 2 * rank, 0:128] = zero
-            ll[g, rank : 2 * rank, 128:256] = leaf[g]
+        double(ll_in, lin_ref, g)
         w = contrast_ref[g : g + 1, :] * fields_ref[g].astype(F32)
         weighted.append(w)
         lhs = jnp.concatenate([w[0:32], w[32:64]], axis=1).astype(BF)
@@ -226,8 +228,6 @@
             s, [adj_ref[g].astype(F32) for g in range(boxes)]
         ).astype(BF)
 
-    loads[5].wait()
-
     def build(i, _):
         l, g = i // boxes, i % boxes
         zero = jnp.zeros((rank, rank), BF)
@@ -238,8 +238,6 @@
             blocks[l, g, rank : 2 * rank, base : base + 128] = jnp.concatenate([zero, m], axis=1)
         return 0
 
-    lax.fori_loop(0, depth * boxes, build, 0)
-
     def inverse(l, s):
         found = 0
         for j in range(1, boxes):
@@ -256,13 +254,22 @@
             bsend[l, s] = carry[l, inverse(l, s)]
         return own
 
-    backs = []
-    for g in range(boxes):
-        a = adj_ref[g]
-        lhs = jnp.concatenate([a[0:32], a[32:64]], axis=1)
-        backs.append(dot(lhs, ll_out[g], NT).astype(BF))
-    own_terms = back_products(depth - 1, backs)
-    acc[...] = jnp.zeros_like(acc)
+    def first_back():
+        loads[4].wait()
+        loads[5].wait()
+        lax.fori_loop((depth - 1) * boxes, depth * boxes, build, 0)
+        backs = []
+        for g in range(boxes):
+            double(ll_out, lout_ref, g)
+            a = adj_ref[g]
+            lhs = jnp.concatenate([a[0:32], a[32:64]], axis=1)
+            backs.append(dot(lhs, ll_out[g], NT).astype(BF))
+        own_terms = back_products(depth - 1, backs)
+        back_copy(depth - 1).start()
+        lax.fori_loop(0, (depth - 1) * boxes, build, 0)
+        acc[...] = jnp.zeros_like(acc)
+        return own_terms
+
 
     def remote(src, dst, sem, device):
         return pltpu.make_async_remote_copy(
@@ -354,20 +361,17 @@
             source = 1 + c % 2 + 2 * (c // 4) - 2 * (c // 5)
             x = column(source - far_edge * (c // 4 - c // 5))
             weight = (1 + near_edge * (1 - (c + 4) // 5)).astype(F32)
+            features = [grid[plane, y, x, 128:144] for y in rows_of]
+            squared = dot(jnp.concatenate(features, axis=1), tgt[goal], TN)
+            values = [grid[plane, y, x, 0:128] for y in rows_of]
             for ty in range(2):
-                target = tgt[3 * ty + goal]
-                values, reals, imags = [], [], []
-                for dy in range(3):
-                    y = rows_of[ty + dy]
-                    values.append(grid[plane, y, x, 0:128])
-                    squared = dot(grid[plane, y, x, 128:144], target, TN)
-                    real, imag = oscillation(squared, scale)
-                    reals.append(real)
-                    imags.append(imag)
-                rhs = jnp.concatenate(
-                    [jnp.concatenate(reals, axis=0), jnp.concatenate(imags, axis=0)], axis=1
+                real, imag = oscillation(
+                    squared[128 * ty : 128 * ty + 384, 128 * ty : 128 * ty + 128], scale
                 )
-                product = dot(jnp.concatenate(values, axis=1), rhs)
+                product = dot(
+                    jnp.concatenate(values[ty : ty + 3], axis=1),
+                    jnp.concatenate([real, imag], axis=1),
+                )
                 acc[3 * ty + goal] = acc[3 * ty + goal] + weight * product
             return 0
 
@@ -386,7 +390,7 @@
     def neighbour_targets():
         for ty in range(2):
             f = grid[1, 1 + ty, 3 - 3 * mirror, 128:144].astype(F32)
-            tgt[3 * ty + 2] = stack(
+            tgt[2, :, 128 * ty : 128 * ty + 128] = stack(
                 [-2.0 * f[0:1], -2.0 * f[1:2], -2.0 * f[2:3], one, one, f[3:4], f[4:5]]
             )
 
@@ -457,7 +461,6 @@
 
     actions = {
         "SF": lambda: forward_copy(0).start(),
-        "SB": lambda: back_copy(depth - 1).start(),
         "SYo": lambda: start(own_y), "RYo": lambda: arrive(own_y),
         "SXo": lambda: start(own_x), "RXo": own_columns,
         "SZ1": lambda: (up_first.start(), down_first.start()),
@@ -487,7 +490,9 @@
             pending.append("omt".index(word[2]) * 6 + c)
             continue
         run_near()
-        if word[0] == "F":
+        if word == "SB":
+            own_terms = first_back()
+        elif word[0] == "F":
             if int(word[1]) < depth:
                 coefs = forward_step(int(word[1]), coefs)
         elif word[0] == "B":
@@ -564,7 +569,7 @@
         scratch_shapes=[pltpu.VMEM(v.shape, v.dtype) for v in inputs]
         + [
             pltpu.VMEM((3, 4, 4, ROWS, points), BF),
-            pltpu.VMEM((6, 16, points), BF),
+            pltpu.VMEM((3, 16, 2 * points), BF),
             pltpu.VMEM((6, 4 * sides, 2 * points), F32),
             pltpu.VMEM((boxes, 2 * rank, 2 * points), BF),
             pltpu.VMEM((boxes, 2 * rank, 2 * points), BF),

time: 77.5 us -> 76.6 us (0.988)
  Pallas kernels: 74.5 us -> 73.6 us
    pallas_call x1, Pallas kernels: 74.5 us -> 73.6 us  [body(): pl.pallas_call(functools.partial(kernel, n_hi, n_lo, scale), out_shape=[j...]
where the time goes in v4:
time: 76.6 us; the launch traced here: 76.4 us
  Pallas kernels  73.6 us (96%)
  local copies, waits for them, and re-layouts  2.14 us (3%)
    pallas_call x1, Pallas kernels, body(): pl.pallas_call(functools.partial(kernel, n_hi, n_lo, scale), out_shape=[j...  73.6 us
    unnamed x4, local copies, waits for them, and re-layouts  2.14 us

profile of v4, /device:TPU:30, one launch (start us, length us, event | category | flops | bytes accessed | tf_op | source)
XLA Modules:
  0.0 76.4 jit_solution(1874788330520428312)
XLA Ops:
  0.6 73.6 %operator.1 = (bf16[4,64,128]{2,1,0:T(8,128)(2,1)}, bf16[4,64,128]{2,1,0:T(8,128)(2,1)}) custom-call(s32[4,8]{1,0:T(4,128)} %bitcast.13, bf16[3,4,128]{2,1,0:T(4,128)(2,1)} %bitcast.12, bf16[4,64,128]{2,1,0:T(8,128)(2,1)} %bitcast.8, bf16[4,64,128]{2,1,0:T(8,128)(2,1)} %bitcast.9, f32[4,128]{1,0:T(4,128)} %refs_2_.1, bf16[4,64,128]{2,1,0:T(8,128)(2,1)} %refs_3_.1, ...), custom_call_target="tpu_custom_call" | custom-call | tf_op jit(solution)/shard_map/operator/pallas_call | solution.py:564
  74.3 0.0 copy-start
  74.3 1.5 %copy.12 = bf16[4,2,32,128]{3,2,1,0:T(8,128)(2,1)} copy(bf16[4,2,32,128]{3,2,1,0:T(8,128)(2,1)} %bitcast.11) | data formatting | bytes 131072
  75.8 0.0 copy-done
  75.8 0.6 copy.13
Async XLA Ops:
  74.3 1.5 %copy-start = (bf16[4,64,128]{2,1,0:T(8,128)(2,1)S(1)}, bf16[4,64,128]{2,1,0:T(8,128)(2,1)}, u32[]{:S(2)}) copy-start(bf16[4,64,128]{2,1,0:T(8,128)(2,1)} %get-tuple-element.5) | copy-start | bytes 196612

commit v5 on v4

--- a/solution.py
+++ b/solution.py
@@ -21,10 +21,10 @@
 
 
 ORDER = (
-    "SF", "SZ1", "SB", "F0", "SYo", "B0", "F1", "RYo", "SXo", "RD", "RU", "B1", "F2", "NAo1",
-    "NAo0", "B2", "Z", "SYm", "SZ2", "NAo2", "F3", "NAo3", "RYm", "SXm", "RZ2", "RXo", "SYt", "F4",
-    "B3", "NAm0", "NAm1", "B4", "NEo", "F5", "NEm", "RYt", "NEt", "ES", "B5", "NAt2", "NAm2", "RXm",
-    "F6", "NAt1", "B6", "SXt", "NAt3", "NAt0", "NAm3", "NCo", "NCm", "F7", "RXt", "NCt", "B7", "ER",
+    "SZ1", "SF", "SB", "F0", "SYo", "B0", "F1", "B1", "RYo", "SXo", "F2", "NAo1", "Z", "SZ2", "B2",
+    "SYm", "NAo0", "NAo3", "NAo2", "F3", "B3", "RYm", "SXm", "RXo", "RZ2", "SYt", "F4", "NAm0",
+    "NEm", "NAm1", "B4", "F5", "NEo", "RYt", "SXt", "NEt", "NAt1", "NAt2", "F6", "ES", "NCo", "B5",
+    "NAm2", "NAm3", "NAt3", "RXm", "B6", "NAt0", "NCm", "F7", "RXt", "NCt", "B7", "ER",
 )
 
 
@@ -76,10 +76,10 @@
     perm_ref, coords_ref, *refs,
 ):
     operands, refs = refs[:6], refs[6:]
-    out_ref, adj_out_ref, *refs = refs
+    out_ref, *refs = refs
     (fields_ref, adj_ref, contrast_ref, lin_ref, lout_ref, mix_ref), refs = refs[:6], refs[6:]
     (
-        grid, tgt, acc, ll_in, ll_out, blocks, fsend, bsend, brecv, carry, relays, res, exsend, exrecv,
+        grid, tgt, acc, ll_in, ll_out, blocks, fsend, bsend, brecv, carry, res, exsend, exrecv,
         send_sem, recv_sem, load_sem, *frecv,
     ) = refs
     loads = [
@@ -134,20 +134,6 @@
     def column(v):
         return v + mirror * (3 - 2 * v)
 
-    ring_bits = list(range(lo_bits + 1, bits)) + [0]
-    ring = 1 << len(ring_bits)
-    zpos = 0
-    for place, bit in enumerate(ring_bits):
-        zpos = zpos + (e // (1 << bit)) % 2 * (1 << place)
-
-    def on_ring(shift):
-        return e - spread(zpos, ring_bits) + spread((zpos + ring + shift) % ring, ring_bits)
-
-    def side(shift):
-        return (zpos + ring + shift) % ring // (ring // 2)
-
-    far_hop = ring // 2 - 1
-
     barrier = pltpu.get_barrier_semaphore()
 
     def greet(device):
@@ -155,8 +141,6 @@
 
     for bit in levels:
         greet(flip(bit))
-    for shift in (far_hop, -far_hop, 1, -1):
-        greet(on_ring(shift))
     others = []
     for d, n, c in ((0, nx, xc), (1, ny, yc)):
         others.append((c > 0, at(d, (c + n - 1) % n)))
@@ -284,18 +268,10 @@
         return remote(bsend.at[l], brecv.at[l], depth + l, flip(levels[l]))
 
     first_sem = 2 * depth
-    last_sem = first_sem + 14
-    up_first = remote(
-        grid.at[1, 1, pl.ds(1, 2)], relays.at[0], first_sem, on_ring(far_hop)
-    )
-    down_first = remote(
-        grid.at[1, 2, pl.ds(1, 2)], relays.at[1], last_sem, on_ring(-far_hop)
-    )
-    up_last = remote(
-        relays.at[0], grid.at[2 * side(-far_hop), 1, pl.ds(1, 2)], last_sem + 1, on_ring(1)
-    )
-    down_last = remote(
-        relays.at[1], grid.at[2 * side(far_hop), 2, pl.ds(1, 2)], last_sem + 2, on_ring(-1)
+    z1 = remote(
+        grid.at[1, pl.ds(1, 2), pl.ds(1, 2)],
+        grid.at[third, pl.ds(1, 2), pl.ds(1, 2)],
+        first_sem, flip(0),
     )
     z2 = remote(
         grid.at[mate, pl.ds(1, 2), pl.ds(1, 2)],
@@ -411,7 +387,7 @@
                 mine = 2 * ty + mirror
                 res[mine] = res[mine] + exrecv[ty].astype(F32)
 
-    peers = depth + 4
+    peers = depth
     for there, _ in others:
         peers = peers + there.astype(jnp.int32)
     pl.semaphore_wait(barrier, peers)
@@ -447,14 +423,6 @@
             for c in copies:
                 action(c)
 
-    def z_last():
-        up_last.wait_recv()
-        down_last.wait_recv()
-
-    def relay(first, last):
-        first.wait_recv()
-        last.start()
-
     def own_columns():
         arrive(own_x)
         neighbour_targets()
@@ -463,9 +431,7 @@
         "SF": lambda: forward_copy(0).start(),
         "SYo": lambda: start(own_y), "RYo": lambda: arrive(own_y),
         "SXo": lambda: start(own_x), "RXo": own_columns,
-        "SZ1": lambda: (up_first.start(), down_first.start()),
-        "RU": lambda: relay(up_first, up_last), "RD": lambda: relay(down_first, down_last),
-        "Z": z_last,
+        "SZ1": lambda: z1.start(), "Z": lambda: z1.wait_recv(),
         "SYm": lambda: start(mate_y), "RYm": lambda: arrive(mate_y),
         "SXm": lambda: start(mate_x), "RXm": lambda: arrive(mate_x),
         "SZ2": lambda: start(z2_copies), "RZ2": lambda: arrive(z2_copies),
@@ -519,20 +485,17 @@
         ).astype(BF)
         far = dot(backs[g], ll_in[g])
         contrast = contrast_ref[g : g + 1, :]
-        adj_out_ref[g, 0:32] = (
+        out_ref[boxes + g, 0:32] = (
             adj_ref[g, 0:32].astype(F32) - contrast * (sums[64:96] + far[:, 0:128])
         ).astype(BF)
-        adj_out_ref[g, 32:64] = (
+        out_ref[boxes + g, 32:64] = (
             adj_ref[g, 32:64].astype(F32) - contrast * (sums[96:128] + far[:, 128:256])
         ).astype(BF)
 
     for l in range(depth):
         forward_copy(l).wait_send()
         back_copy(l).wait_send()
-    up_first.wait_send()
-    down_first.wait_send()
-    up_last.wait_send()
-    down_last.wait_send()
+    z1.wait_send()
     sent(z2_copies)
     sent(own_y)
     sent(own_x)
@@ -556,16 +519,16 @@
     smem = pl.BlockSpec(memory_space=pltpu.SMEM)
     away = pl.BlockSpec(memory_space=pl.ANY)
     flat = (boxes, parts * sides, points)
-    copies = 2 * depth + 17
+    copies = 2 * depth + 14
     level = (depth, boxes, sides, 2 * rank)
     inputs = (
         fields.reshape(flat), adjoint_in.reshape(flat), contrast, leaf_in, leaf_out, mixing,
     )
     out = pl.pallas_call(
         functools.partial(kernel, n_hi, n_lo, scale),
-        out_shape=[jax.ShapeDtypeStruct(flat, BF)] * 2,
+        out_shape=jax.ShapeDtypeStruct((2 * boxes,) + flat[1:], BF),
         in_specs=[smem, vmem] + [away] * 6,
-        out_specs=[vmem] * 2,
+        out_specs=vmem,
         scratch_shapes=[pltpu.VMEM(v.shape, v.dtype) for v in inputs]
         + [
             pltpu.VMEM((3, 4, 4, ROWS, points), BF),
@@ -578,7 +541,6 @@
             pltpu.VMEM(level, BF),
             pltpu.VMEM(level, BF),
             pltpu.VMEM(level, BF),
-            pltpu.VMEM((2, 2, ROWS, points), BF),
             pltpu.VMEM((boxes, 4 * sides, points), F32),
             pltpu.VMEM((2, 4 * sides, points), BF),
             pltpu.VMEM((2, 4 * sides, points), BF),
@@ -596,7 +558,7 @@
         coords.swapaxes(0, 1),
         *inputs,
     )
-    return (out[0].reshape(fields.shape), out[1].reshape(fields.shape))
+    return (out[:boxes].reshape(fields.shape), out[boxes:].reshape(fields.shape))
 
 
 def solution(mesh):

time: 76.6 us -> 80.3 us (1.048)
  the two profiles are of different devices: /device:TPU:30 before, /device:TPU:4 now
where the time goes in v5:
time: 80.3 us; the launch traced here: 80.1 us
  Pallas kernels  78 us (97%)
  local copies, waits for them, and re-layouts  1.53 us (2%)
    pallas_call x1, Pallas kernels, body(): pl.pallas_call(functools.partial(kernel, n_hi, n_lo, scale), out_shape=ja...  78 us

profile of v5, /device:TPU:4, one launch (start us, length us, event | category | flops | bytes accessed | tf_op | source)
XLA Modules:
  0.0 80.1 jit_solution(18111338660277184297)
XLA Ops:
  0.6 78.0 %operator.1 = bf16[8,64,128]{2,1,0:T(8,128)(2,1)} custom-call(s32[4,8]{1,0:T(4,128)} %bitcast.13, bf16[3,4,128]{2,1,0:T(4,128)(2,1)} %bitcast.12, bf16[4,64,128]{2,1,0:T(8,128)(2,1)} %bitcast.8, bf16[4,64,128]{2,1,0:T(8,128)(2,1)} %bitcast.9, f32[4,128]{1,0:T(4,128)} %refs_2_.1, bf16[4,64,128]{2,1,0:T(8,128)(2,1)} %refs_3_.1, bf16[4,64,128]{2,1,0:T(8,128)(2,1)} %refs_4_.1, ...), custom_call_target="tpu_custom_call" | custom-call | tf_op jit(solution)/shard_map/operator/pallas_call | solution.py:527
  78.6 1.5 %fusion = (bf16[4,64,128]{2,1,0:T(8,128)(2,1)}, bf16[4,64,128]{2,1,0:T(8,128)(2,1)}) fusion(bf16[8,64,128]{2,1,0:T(8,128)(2,1)} %operator.1), kind=kLoop, calls=%fused_computation | loop fusion | bytes 262144 | tf_op jit(solution)/shard_map/slice | solution.py:561

commit v6 on v4

--- a/solution.py
+++ b/solution.py
@@ -21,10 +21,11 @@
 
 
 ORDER = (
-    "SF", "SZ1", "SB", "F0", "SYo", "B0", "F1", "RYo", "SXo", "RD", "RU", "B1", "F2", "NAo1",
-    "NAo0", "B2", "Z", "SYm", "SZ2", "NAo2", "F3", "NAo3", "RYm", "SXm", "RZ2", "RXo", "SYt", "F4",
-    "B3", "NAm0", "NAm1", "B4", "NEo", "F5", "NEm", "RYt", "NEt", "ES", "B5", "NAt2", "NAm2", "RXm",
-    "F6", "NAt1", "B6", "SXt", "NAt3", "NAt0", "NAm3", "NCo", "NCm", "F7", "RXt", "NCt", "B7", "ER",
+    "SZ1", "SF", "SB", "FR", "SYo", "B0", "F0", "F1", "RYo", "SXo", "RD", "RU", "B1", "F2", "NAo1",
+    "B2", "Z", "SZ2", "SYm", "NAo0", "B3", "NAo2", "F3", "NAo3", "RYm", "SXm", "RZ2", "SYt", "F4",
+    "NAm2", "RXo", "NAm0", "NAm3", "NAm1", "B4", "F5", "NEo", "RYt", "SXt", "NEt", "NEm", "B5",
+    "F6", "NAt2", "NAt1", "B6", "NAt3", "RXm", "NAt0", "ES", "NCo", "NCm", "BR", "F7", "RXt", "NCt",
+    "B7", "ER",
 )
 
 
@@ -76,10 +77,10 @@
     perm_ref, coords_ref, *refs,
 ):
     operands, refs = refs[:6], refs[6:]
-    out_ref, adj_out_ref, *refs = refs
+    out_ref, *refs = refs
     (fields_ref, adj_ref, contrast_ref, lin_ref, lout_ref, mix_ref), refs = refs[:6], refs[6:]
     (
-        grid, tgt, acc, ll_in, ll_out, blocks, fsend, bsend, brecv, carry, relays, res, exsend, exrecv,
+        grid, tgt, acc, ll_in, ll_out, blocks, fsend, bsend, brecv, carry, relays, f_stop, b_stop, res, exsend, exrecv,
         send_sem, recv_sem, load_sem, *frecv,
     ) = refs
     loads = [
@@ -297,6 +298,35 @@
     down_last = remote(
         relays.at[1], grid.at[2 * side(far_hop), 2, pl.ds(1, 2)], last_sem + 2, on_ring(-1)
     )
+    half = boxes // 2
+
+    def halves(src, stop, dst, sem):
+        first = (
+            remote(src.at[pl.ds(0, half)], stop.at[0], sem, on_ring(far_hop)),
+            remote(src.at[pl.ds(half, half)], stop.at[1], sem + 1, on_ring(-far_hop)),
+        )
+        last = (
+            remote(stop.at[0], dst.at[pl.ds(0, half)], sem + 2, on_ring(1)),
+            remote(stop.at[1], dst.at[pl.ds(half, half)], sem + 3, on_ring(-1)),
+        )
+        return first, last
+
+    f_first, f_last = halves(fsend.at[0], f_stop, frecv[0], last_sem + 3)
+    b_first, b_last = halves(bsend.at[0], b_stop, brecv.at[0], last_sem + 7)
+
+    def start_all(copies):
+        for copy in copies:
+            copy.start()
+
+    def arrive_all(copies):
+        for copy in copies:
+            copy.wait_recv()
+
+    def relay_all(first, last):
+        for before, after in zip(first, last):
+            before.wait_recv()
+            after.start()
+
     z2 = remote(
         grid.at[mate, pl.ds(1, 2), pl.ds(1, 2)],
         grid.at[third, pl.ds(1, 2), pl.ds(1, 2)],
@@ -420,7 +450,10 @@
 
     def forward_step(i, coefs):
         mine = [dot(coefs[g], blocks[i, g, :, 0:128], NT) for g in range(boxes)]
-        forward_copy(i).wait_recv()
+        if i == 0:
+            arrive_all(f_last)
+        else:
+            forward_copy(i).wait_recv()
         new = []
         for g in range(boxes):
             arrived = frecv[i][perm_ref[g, i]]
@@ -434,11 +467,17 @@
 
     def back_step(i, own_terms):
         l = depth - 1 - i
-        back_copy(l).wait_recv()
+        if l == 0:
+            arrive_all(b_last)
+        else:
+            back_copy(l).wait_recv()
         backs = [(own_terms[g] + brecv[l, g].astype(F32)).astype(BF) for g in range(boxes)]
         if l > 0:
             own_terms = back_products(l - 1, backs)
-            back_copy(l - 1).start()
+            if l == 1:
+                start_all(b_first)
+            else:
+                back_copy(l - 1).start()
         return backs, own_terms
 
     def when_third(action, *copies):
@@ -460,7 +499,8 @@
         neighbour_targets()
 
     actions = {
-        "SF": lambda: forward_copy(0).start(),
+        "SF": lambda: start_all(f_first),
+        "FR": lambda: relay_all(f_first, f_last), "BR": lambda: relay_all(b_first, b_last),
         "SYo": lambda: start(own_y), "RYo": lambda: arrive(own_y),
         "SXo": lambda: start(own_x), "RXo": own_columns,
         "SZ1": lambda: (up_first.start(), down_first.start()),
@@ -492,14 +532,14 @@
         run_near()
         if word == "SB":
             own_terms = first_back()
+        elif word in actions:
+            actions[word]()
         elif word[0] == "F":
             if int(word[1]) < depth:
                 coefs = forward_step(int(word[1]), coefs)
         elif word[0] == "B":
             if int(word[1]) < depth:
                 backs, own_terms = back_step(int(word[1]), own_terms)
-        else:
-            actions[word]()
     run_near()
 
     def pick_raster(g):
@@ -519,16 +559,18 @@
         ).astype(BF)
         far = dot(backs[g], ll_in[g])
         contrast = contrast_ref[g : g + 1, :]
-        adj_out_ref[g, 0:32] = (
+        out_ref[boxes + g, 0:32] = (
             adj_ref[g, 0:32].astype(F32) - contrast * (sums[64:96] + far[:, 0:128])
         ).astype(BF)
-        adj_out_ref[g, 32:64] = (
+        out_ref[boxes + g, 32:64] = (
             adj_ref[g, 32:64].astype(F32) - contrast * (sums[96:128] + far[:, 128:256])
         ).astype(BF)
 
-    for l in range(depth):
+    for l in range(1, depth):
         forward_copy(l).wait_send()
         back_copy(l).wait_send()
+    for copy in f_first + f_last + b_first + b_last:
+        copy.wait_send()
     up_first.wait_send()
     down_first.wait_send()
     up_last.wait_send()
@@ -556,16 +598,16 @@
     smem = pl.BlockSpec(memory_space=pltpu.SMEM)
     away = pl.BlockSpec(memory_space=pl.ANY)
     flat = (boxes, parts * sides, points)
-    copies = 2 * depth + 17
+    copies = 2 * depth + 25
     level = (depth, boxes, sides, 2 * rank)
     inputs = (
         fields.reshape(flat), adjoint_in.reshape(flat), contrast, leaf_in, leaf_out, mixing,
     )
     out = pl.pallas_call(
         functools.partial(kernel, n_hi, n_lo, scale),
-        out_shape=[jax.ShapeDtypeStruct(flat, BF)] * 2,
+        out_shape=jax.ShapeDtypeStruct((2 * boxes,) + flat[1:], BF),
         in_specs=[smem, vmem] + [away] * 6,
-        out_specs=[vmem] * 2,
+        out_specs=vmem,
         scratch_shapes=[pltpu.VMEM(v.shape, v.dtype) for v in inputs]
         + [
             pltpu.VMEM((3, 4, 4, ROWS, points), BF),
@@ -579,6 +621,8 @@
             pltpu.VMEM(level, BF),
             pltpu.VMEM(level, BF),
             pltpu.VMEM((2, 2, ROWS, points), BF),
+            pltpu.VMEM((2, 2) + level[2:], BF),
+            pltpu.VMEM((2, 2) + level[2:], BF),
             pltpu.VMEM((boxes, 4 * sides, points), F32),
             pltpu.VMEM((2, 4 * sides, points), BF),
             pltpu.VMEM((2, 4 * sides, points), BF),
@@ -596,7 +640,7 @@
         coords.swapaxes(0, 1),
         *inputs,
     )
-    return (out[0].reshape(fields.shape), out[1].reshape(fields.shape))
+    return (out[:boxes].reshape(fields.shape), out[boxes:].reshape(fields.shape))
 
 
 def solution(mesh):

time: 76.6 us -> 82.4 us (1.076)
  the two profiles are of different devices: /device:TPU:30 before, /device:TPU:25 now
where the time goes in v6:
time: 82.4 us; the launch traced here: 82.2 us
  Pallas kernels  80 us (97%)
  local copies, waits for them, and re-layouts  1.53 us (2%)
    pallas_call x1, Pallas kernels, body(): pl.pallas_call(functools.partial(kernel, n_hi, n_lo, scale), out_shape=ja...  80 us

profile of v6, /device:TPU:25, one launch (start us, length us, event | category | flops | bytes accessed | tf_op | source)
XLA Modules:
  0.0 82.2 jit_solution(12092642614328204678)
XLA Ops:
  0.6 80.0 %operator.1 = bf16[8,64,128]{2,1,0:T(8,128)(2,1)} custom-call(s32[4,8]{1,0:T(4,128)} %bitcast.13, bf16[3,4,128]{2,1,0:T(4,128)(2,1)} %bitcast.12, bf16[4,64,128]{2,1,0:T(8,128)(2,1)} %bitcast.8, bf16[4,64,128]{2,1,0:T(8,128)(2,1)} %bitcast.9, f32[4,128]{1,0:T(4,128)} %refs_2_.1, bf16[4,64,128]{2,1,0:T(8,128)(2,1)} %refs_3_.1, bf16[4,64,128]{2,1,0:T(8,128)(2,1)} %refs_4_.1, ...), custom_call_target="tpu_custom_call" | custom-call | tf_op jit(solution)/shard_map/operator/pallas_call | solution.py:606
  80.6 1.5 %fusion = (bf16[4,64,128]{2,1,0:T(8,128)(2,1)}, bf16[4,64,128]{2,1,0:T(8,128)(2,1)}) fusion(bf16[8,64,128]{2,1,0:T(8,128)(2,1)} %operator.1), kind=kLoop, calls=%fused_computation | loop fusion | bytes 262144 | tf_op jit(solution)/shard_map/slice | solution.py:643

commit v7 on v4

--- a/solution.py
+++ b/solution.py
@@ -21,10 +21,11 @@
 
 
 ORDER = (
-    "SF", "SZ1", "SB", "F0", "SYo", "B0", "F1", "RYo", "SXo", "RD", "RU", "B1", "F2", "NAo1",
-    "NAo0", "B2", "Z", "SYm", "SZ2", "NAo2", "F3", "NAo3", "RYm", "SXm", "RZ2", "RXo", "SYt", "F4",
-    "B3", "NAm0", "NAm1", "B4", "NEo", "F5", "NEm", "RYt", "NEt", "ES", "B5", "NAt2", "NAm2", "RXm",
-    "F6", "NAt1", "B6", "SXt", "NAt3", "NAt0", "NAm3", "NCo", "NCm", "F7", "RXt", "NCt", "B7", "ER",
+    "SF", "SB", "SZ1", "F0", "SYo", "B0", "F1", "RYo", "RU", "RD", "SXo", "NAo2", "B1", "F2",
+    "NAo1", "Z", "SYm", "B2", "SZ2", "NAo0", "F3", "RXo", "NEo", "NAo3", "B3", "RZ2", "SYt", "RYm",
+    "F4", "NCo", "SXm", "NEm", "NAm0", "B4", "F5", "RYt", "NAm3", "NEt", "SXt", "B5", "F6", "NAm2",
+    "NAt1", "NAm1", "B6", "ES", "NAt3", "RXt", "RXm", "NAt2", "F7", "NCt", "NCm", "NAt0", "B7",
+    "ER",
 )
 
 
@@ -76,7 +77,7 @@
     perm_ref, coords_ref, *refs,
 ):
     operands, refs = refs[:6], refs[6:]
-    out_ref, adj_out_ref, *refs = refs
+    out_ref, *refs = refs
     (fields_ref, adj_ref, contrast_ref, lin_ref, lout_ref, mix_ref), refs = refs[:6], refs[6:]
     (
         grid, tgt, acc, ll_in, ll_out, blocks, fsend, bsend, brecv, carry, relays, res, exsend, exrecv,
@@ -519,10 +520,10 @@
         ).astype(BF)
         far = dot(backs[g], ll_in[g])
         contrast = contrast_ref[g : g + 1, :]
-        adj_out_ref[g, 0:32] = (
+        out_ref[boxes + g, 0:32] = (
             adj_ref[g, 0:32].astype(F32) - contrast * (sums[64:96] + far[:, 0:128])
         ).astype(BF)
-        adj_out_ref[g, 32:64] = (
+        out_ref[boxes + g, 32:64] = (
             adj_ref[g, 32:64].astype(F32) - contrast * (sums[96:128] + far[:, 128:256])
         ).astype(BF)
 
@@ -563,9 +564,9 @@
     )
     out = pl.pallas_call(
         functools.partial(kernel, n_hi, n_lo, scale),
-        out_shape=[jax.ShapeDtypeStruct(flat, BF)] * 2,
+        out_shape=jax.ShapeDtypeStruct((2 * boxes,) + flat[1:], BF),
         in_specs=[smem, vmem] + [away] * 6,
-        out_specs=[vmem] * 2,
+        out_specs=vmem,
         scratch_shapes=[pltpu.VMEM(v.shape, v.dtype) for v in inputs]
         + [
             pltpu.VMEM((3, 4, 4, ROWS, points), BF),
@@ -596,7 +597,7 @@
         coords.swapaxes(0, 1),
         *inputs,
     )
-    return (out[0].reshape(fields.shape), out[1].reshape(fields.shape))
+    return (out[:boxes].reshape(fields.shape), out[boxes:].reshape(fields.shape))
 
 
 def solution(mesh):

time: 76.6 us -> 75.2 us (0.982)
  the two profiles are of different devices: /device:TPU:30 before, /device:TPU:25 now
where the time goes in v7:
time: 75.2 us; the launch traced here: 74.1 us
  Pallas kernels  71.9 us (96%)
  local copies, waits for them, and re-layouts  1.53 us (2%)
    pallas_call x1, Pallas kernels, body(): pl.pallas_call(functools.partial(kernel, n_hi, n_lo, scale), out_shape=ja...  71.9 us
    slice x1, local copies, waits for them, and re-layouts, body(): out[boxes:].reshape(fields.shape)  1.53 us

profile of v7, /device:TPU:25, one launch (start us, length us, event | category | flops | bytes accessed | tf_op | source)
XLA Modules:
  0.0 74.1 jit_solution(5283830881371630304)
XLA Ops:
  0.6 71.9 %operator.1 = bf16[8,64,128]{2,1,0:T(8,128)(2,1)} custom-call(s32[4,8]{1,0:T(4,128)} %bitcast.13, bf16[3,4,128]{2,1,0:T(4,128)(2,1)} %bitcast.12, bf16[4,64,128]{2,1,0:T(8,128)(2,1)} %bitcast.8, bf16[4,64,128]{2,1,0:T(8,128)(2,1)} %bitcast.9, f32[4,128]{1,0:T(4,128)} %refs_2_.1, bf16[4,64,128]{2,1,0:T(8,128)(2,1)} %refs_3_.1, bf16[4,64,128]{2,1,0:T(8,128)(2,1)} %refs_4_.1, ...), custom_call_target="tpu_custom_call" | custom-call | tf_op jit(solution)/shard_map/operator/pallas_call | solution.py:565
  72.5 1.5 %fusion = (bf16[4,64,128]{2,1,0:T(8,128)(2,1)}, bf16[4,64,128]{2,1,0:T(8,128)(2,1)}) fusion(bf16[8,64,128]{2,1,0:T(8,128)(2,1)} %operator.1), kind=kLoop, calls=%fused_computation | loop fusion | bytes 262144 | tf_op jit(solution)/shard_map/slice | solution.py:600

commit v8 on v7

--- a/solution.py
+++ b/solution.py
@@ -21,7 +21,7 @@
 
 
 ORDER = (
-    "SF", "SB", "SZ1", "F0", "SYo", "B0", "F1", "RYo", "RU", "RD", "SXo", "NAo2", "B1", "F2",
+    "SF", "SB", "SZ1", "P", "F0", "SYo", "B0", "F1", "RYo", "RU", "RD", "SXo", "NAo2", "B1", "F2",
     "NAo1", "Z", "SYm", "B2", "SZ2", "NAo0", "F3", "RXo", "NEo", "NAo3", "B3", "RZ2", "SYt", "RYm",
     "F4", "NCo", "SXm", "NEm", "NAm0", "B4", "F5", "RYt", "NAm3", "NEt", "SXt", "B5", "F6", "NAm2",
     "NAt1", "NAm1", "B6", "ES", "NAt3", "RXt", "RXm", "NAt2", "F7", "NCt", "NCm", "NAt0", "B7",
@@ -258,7 +258,7 @@
     def first_back():
         loads[4].wait()
         loads[5].wait()
-        lax.fori_loop((depth - 1) * boxes, depth * boxes, build, 0)
+        lax.fori_loop((depth - 1) * boxes, depth * boxes, build, 0, unroll=boxes)
         backs = []
         for g in range(boxes):
             double(ll_out, lout_ref, g)
@@ -267,9 +267,11 @@
             backs.append(dot(lhs, ll_out[g], NT).astype(BF))
         own_terms = back_products(depth - 1, backs)
         back_copy(depth - 1).start()
-        lax.fori_loop(0, (depth - 1) * boxes, build, 0)
+        return own_terms
+
+    def other_blocks():
+        lax.fori_loop(0, (depth - 1) * boxes, build, 0, unroll=boxes)
         acc[...] = jnp.zeros_like(acc)
-        return own_terms
 
 
     def remote(src, dst, sem, device):
@@ -472,7 +474,7 @@
         "SZ2": lambda: start(z2_copies), "RZ2": lambda: arrive(z2_copies),
         "SYt": lambda: when_third(start, third_y), "RYt": lambda: when_third(arrive, third_y),
         "SXt": lambda: when_third(start, third_x), "RXt": lambda: when_third(arrive, third_x),
-        "ES": send_extra, "ER": receive_extra,
+        "ES": send_extra, "ER": receive_extra, "P": other_blocks,
     }
     pending = []
 

time: 75.2 us -> 75.9 us (level)
  the two profiles are of different devices: /device:TPU:25 before, /device:TPU:3 now
where the time goes in v8:
time: 75.9 us; the launch traced here: 75.7 us
  Pallas kernels  73.5 us (97%)
  local copies, waits for them, and re-layouts  1.53 us (2%)
    pallas_call x1, Pallas kernels, body(): pl.pallas_call(functools.partial(kernel, n_hi, n_lo, scale), out_shape=ja...  73.5 us
    slice x1, local copies, waits for them, and re-layouts, body(): out[boxes:].reshape(fields.shape)  1.53 us

profile of v8, /device:TPU:3, one launch (start us, length us, event | category | flops | bytes accessed | tf_op | source)
XLA Modules:
  0.0 75.7 jit_solution(3779163748851733890)
XLA Ops:
  0.6 73.5 %operator.1 = bf16[8,64,128]{2,1,0:T(8,128)(2,1)} custom-call(s32[4,8]{1,0:T(4,128)} %bitcast.13, bf16[3,4,128]{2,1,0:T(4,128)(2,1)} %bitcast.12, bf16[4,64,128]{2,1,0:T(8,128)(2,1)} %bitcast.8, bf16[4,64,128]{2,1,0:T(8,128)(2,1)} %bitcast.9, f32[4,128]{1,0:T(4,128)} %refs_2_.1, bf16[4,64,128]{2,1,0:T(8,128)(2,1)} %refs_3_.1, bf16[4,64,128]{2,1,0:T(8,128)(2,1)} %refs_4_.1, ...), custom_call_target="tpu_custom_call" | custom-call | tf_op jit(solution)/shard_map/operator/pallas_call | solution.py:567
  74.2 1.5 %fusion = (bf16[4,64,128]{2,1,0:T(8,128)(2,1)}, bf16[4,64,128]{2,1,0:T(8,128)(2,1)}) fusion(bf16[8,64,128]{2,1,0:T(8,128)(2,1)} %operator.1), kind=kLoop, calls=%fused_computation | loop fusion | bytes 262144 | tf_op jit(solution)/shard_map/slice | solution.py:602
